TPU v7x, 256 devices: a whole 4x4x8 slice. The times are simulated.
256 devices in a mesh: seq: 128 (over x_hi, z, y, core), tp: 2 (over x_lo).
Axes of the slice: x: 4 (x_hi: 2, x_lo: 2; x = x_hi * 2 + x_lo), y: 4, z: 8, core: 2. Of those that a mesh axis runs over, the one named last changes fastest.
Arguments:
- residual_in: bfloat16 [32768, 1024], P('seq', 'tp'), may hold values from -6 to 6
- queries: bfloat16 [32768, 1024], P('seq', 'tp'), may hold values from -240 to 240
- keys: bfloat16 [32768, 1024], P('seq', 'tp'), may hold values from -12 to 12
- values: bfloat16 [32768, 1024], P('seq', 'tp'), may hold values from -6 to 6
- head_offset: int32 [6, 16], P(None, 'tp'), may hold values from 0 to 31
- out_weight: bfloat16 [1024, 1024], P('tp'), may hold values from -0.1875 to 0.1875
- norm_gain: float32 [1024], replicated, may hold values from 0.5 to 1.5
- gate_weight: bfloat16 [1024, 2048], P(None, 'tp'), may hold values from -0.1875 to 0.1875
- up_weight: bfloat16 [1024, 2048], P(None, 'tp'), may hold values from -0.1875 to 0.1875
- down_weight: bfloat16 [2048, 1024], P('tp'), may hold values from -0.125 to 0.125
Outputs:
- layer_out: bfloat16 [32768, 1024], P('seq', 'tp')
All inputs are finite; a program needn't handle non-finite values.
Results may differ from a plain program's by a relative error of at most 0.0095.
Values may be sent and summed in bfloat16 or wider, within the bound.
A program may use at most 128 MiB of HBM per device.

v0:
```python
import math

import jax
import jax.numpy as jnp
from jax import lax
from jax.sharding import PartitionSpec as P

BRANCHES = 6


masked_score = -1e30


def from_partner(block, axis, distance):
    count = lax.axis_size(axis)
    route = []
    for low in range(count):
        high = low | 1 << distance
        if high != low and high < count:
            route += [(low, high), (high, low)]
    return lax.ppermute(block, axis, route)


def pick_rows(array, choose, rate):
    count = array.shape[0] // rate
    shaped = array.reshape(count, rate, array.shape[1], array.shape[2])
    return jnp.sum(shaped * choose[None, :, :, None].astype(array.dtype), axis=1)


def place_bit(blocks, partner, upper):
    first = jnp.where(upper, partner, blocks)
    second = jnp.where(upper, blocks, partner)
    return jnp.concatenate([first, second], axis=0)


def shards(
    residual_in,
    queries,
    keys,
    values,
    head_offset,
    out_weight,
    norm_gain,
    gate_weight,
    up_weight,
    down_weight,
):
    rows = queries.shape[0]
    cols = queries.shape[1]
    heads_here = head_offset.shape[1]
    head_dim = cols // heads_here
    seq_count = lax.axis_size("seq")
    seq_index = lax.axis_index("seq")
    top_bits = min(seq_count.bit_length() - 1, BRANCHES)
    scale = 1.0 / math.sqrt(head_dim)
    query_heads = queries.reshape(rows, heads_here, head_dim)
    key_heads = keys.reshape(rows, heads_here, head_dim)
    value_heads = values.reshape(rows, heads_here, head_dim)
    order = list(range(top_bits))
    chooses = []
    picked_queries = []
    stacks = []
    bit_counts = []
    for branch in range(BRANCHES):
        rate = 2**branch
        offsets = head_offset[branch] % rate
        choose = jnp.arange(rate, dtype=jnp.int32)[:, None] == offsets[None, :]
        chooses.append(choose)
        picked_queries.append(pick_rows(query_heads, choose, rate))
        picked_key = pick_rows(key_heads, choose, rate).reshape(rows // rate, cols)
        picked_value = pick_rows(value_heads, choose, rate).reshape(rows // rate, cols)
        stacks.append(jnp.concatenate([picked_key, picked_value], axis=1)[None])
        bit_counts.append(min(branch + 1, top_bits))
    for branch in range(BRANCHES):
        blocks = stacks[branch]
        for bit in order:
            if bit < bit_counts[branch]:
                partner = from_partner(blocks, "seq", bit)
                blocks = place_bit(blocks, partner, seq_index // 2**bit % 2 == 1)
        stacks[branch] = blocks
    peak = None
    total = None
    accum = None
    for branch in range(BRANCHES):
        rate = 2**branch
        group = 2 ** bit_counts[branch]
        count = rows // rate
        whole = stacks[branch].reshape(group * count, 2 * cols)
        key_rows = whole[:, :cols].reshape(group * count, heads_here, head_dim).transpose(1, 0, 2)
        value_rows = whole[:, cols:].reshape(group * count, heads_here, head_dim).transpose(1, 0, 2)
        query_rows = picked_queries[branch].transpose(1, 0, 2)
        position = seq_index % group * count + jnp.arange(count, dtype=jnp.int32)
        causal = jnp.arange(group * count, dtype=jnp.int32)[None, :] <= position[:, None]

        def attend(block):
            query, key_block, value_block = block
            scores = jnp.dot(query, key_block.T, preferred_element_type=jnp.float32) * scale
            scores = jnp.where(causal, scores, masked_score)
            top = jnp.max(scores, axis=1, keepdims=True)
            log_total = top + jnp.log(jnp.sum(jnp.exp(scores - top), axis=1, keepdims=True))
            weights = jnp.exp(scores - log_total).astype(jnp.bfloat16)
            output = jnp.dot(weights, value_block, preferred_element_type=jnp.float32)
            return (output, log_total[:, 0])

        outputs, logs = lax.map(attend, (query_rows, key_rows, value_rows))
        choose = chooses[branch]
        chosen = choose.astype(jnp.float32)
        spread = (outputs.transpose(1, 0, 2)[:, None] * chosen[None, :, :, None]).reshape(
            rows, heads_here, head_dim
        )
        spread_log = jnp.broadcast_to(logs.T[:, None, :], (count, rate, heads_here)).reshape(
            rows, heads_here
        )
        covered = jnp.broadcast_to(choose[None], (count, rate, heads_here)).reshape(
            rows, heads_here
        )
        if branch == 0:
            peak = spread_log
            total = jnp.ones((rows, heads_here), jnp.float32)
            accum = spread
        else:
            new_peak = jnp.where(covered, jnp.maximum(peak, spread_log), peak)
            keep = jnp.exp(peak - new_peak)
            branch_weight = jnp.where(
                covered, jnp.exp(jnp.where(covered, spread_log, new_peak) - new_peak), 0.0
            )
            total = total * keep + branch_weight
            accum = accum * keep[..., None] + branch_weight[..., None] * spread
            peak = new_peak
    mix = (accum / total[..., None]).astype(jnp.bfloat16).reshape(rows, cols)
    partial_value = jnp.dot(mix, out_weight, preferred_element_type=jnp.float32)
    width = residual_in.shape[1]
    start = lax.axis_index("tp") * width
    model_width = norm_gain.shape[0]
    share = lax.psum_scatter(
        partial_value, "tp", scatter_dimension=1, tiled=True
    ) + residual_in.astype(jnp.float32)
    squares = lax.psum(jnp.sum(share * share, axis=1), "tp")
    inverse = lax.rsqrt(squares / model_width + 1e-05)
    gain_share = lax.dynamic_slice_in_dim(norm_gain, start, width)
    normed = (share * inverse[:, None] * gain_share[None, :]).astype(jnp.bfloat16)
    piece = lax.all_gather(normed, "tp", axis=1, tiled=True)
    gate = jnp.dot(piece, gate_weight, preferred_element_type=jnp.float32)
    up = jnp.dot(piece, up_weight, preferred_element_type=jnp.float32)
    act = (jax.nn.silu(gate) * up).astype(jnp.bfloat16)
    ffn = lax.psum_scatter(
        jnp.dot(act, down_weight, preferred_element_type=jnp.float32).astype(jnp.bfloat16),
        "tp",
        scatter_dimension=1,
        tiled=True,
    ).astype(jnp.float32)
    return (share + ffn).astype(jnp.bfloat16)


def solution(mesh):
    placed = (
        P("seq", "tp"),
        P("seq", "tp"),
        P("seq", "tp"),
        P("seq", "tp"),
        P(None, "tp"),
        P("tp", None),
        P(),
        P(None, "tp"),
        P(None, "tp"),
        P("tp", None),
    )
    return jax.shard_map(
        shards, mesh=mesh, in_specs=placed, out_specs=P("seq", "tp"), check_vma=False
    )
```

profile of v0, /device:TPU:1, one launch (start us, length us, event | category | flops | bytes accessed | tf_op | source)
XLA Modules:
  0.0 366.1 jit_solution(1349763704975447843)
XLA Ops:
  6.5 1.5 fusion.110
  9.8 2.1 reshape_reshape.52
  11.9 2.1 reshape_reshape.53
  14.0 2.9 multiply_reduce_fusion.14
  20.0 3.2 collective-permute-start.1
  26.2 2.8 multiply_reduce_fusion.11
  34.9 2.5 multiply_reduce_fusion.8
  43.5 2.3 multiply_reduce_fusion.5
  51.9 2.3 multiply_reduce_fusion.2
  64.2 1.4 copy.232
  71.1 1.3 copy.241
  82.5 1.9 collective-permute-done.16
  84.5 2.3 collective-permute-start.17
  87.8 1.4 collective-permute-done.17
  89.2 2.4 collective-permute-start.12
  91.6 1.6 collective-permute-start.18
  94.8 2.8 collective-permute-start.8
  97.6 1.4 collective-permute-start.13
  99.1 3.1 collective-permute-start.19
  106.0 2.1 collective-permute-start.5
  110.7 2.8 collective-permute-start.14
  114.4 4.7 %collective-permute-start.20 = (bf16[32,8,1024]{2,1,0:T(8,128)(2,1)}, bf16[32,8,1024]{2,1,0:T(8,128)(2,1)}, u32[]{:S(2)}, u32[]{:S(2)}) collective-permute-start(bf16[32,8,1024]{2,1,0:T(8,128)(2,1)} %pad_maximum_fusion.9), channel_id=1, source_target_pairs={{0,64},{64,0},{2,66},{66,2},{4,68},{68,4},{6,70},{70,6},{8,72},{72... | collective-permute-start | bytes 1572872 | tf_op jit(solution)/shard_map/ppermute | solution.py:21
  120.4 2.0 copy.261
  123.4 36.0 %while.78 = (s32[]{:T(128)}, f32[8,256,64]{1,2,0:T(8,128)}, f32[8,256]{1,0:T(8,128)}, bf16[8,256,64]{1,2,0:T(8,128)(2,1)}, bf16[8,512,64]{1,2,0:T(8,128)(2,1)}, ...) while((s32[]{:T(128)}, f32[8,256,64]{1,2,0:T(8,128)}, ...), condition=%wide.region_3.4_spmd.clone, body=%wide.region_0.0_spmd.clone.sunk | while | flops 34602752 | bytes 1814625 | solution.py:105
  124.9 1.8 fusion.173
  126.7 1.3 dynamic_update_slice.79
  129.4 1.8 fusion.173
  131.1 1.3 dynamic_update_slice.79
  133.9 1.8 fusion.173
  135.6 1.3 dynamic_update_slice.79
  138.4 1.8 fusion.173
  140.1 1.3 dynamic_update_slice.79
  142.9 1.8 fusion.173
  144.6 1.3 dynamic_update_slice.79
  147.4 1.8 fusion.173
  149.1 1.3 dynamic_update_slice.79
  151.9 1.8 fusion.173
  153.6 1.3 dynamic_update_slice.79
  156.3 1.8 fusion.173
  158.1 1.3 dynamic_update_slice.79
  161.6 1.5 copy.192
  166.7 17.0 %while.79 = (s32[]{:T(128)}, f32[8,128,64]{1,2,0:T(8,128)}, f32[8,128]{1,0:T(8,128)S(1)}, bf16[8,128,64]{2,1,0:T(8,128)(2,1)}, bf16[8,512,64]{1,2,0:T(8,128)(2,1...) while((s32[]{:T(128)}, f32[8,128,64]{1,2,0:T(8,128)}, ...), condition=%wide.region_10.11_spmd.clone, body=%wide.region_7.0_spmd.clone.sunk | while | flops 17301376 | bytes 990305 | solution.py:105
  183.9 2.0 copy.204
  188.1 2.0 copy.206
  192.8 17.5 %while.80 = (s32[]{:T(128)}, f32[8,64,64]{2,1,0:T(8,128)}, f32[8,64]{1,0:T(8,128)S(1)}, bf16[8,64,64]{2,1,0:T(8,128)(2,1)}, bf16[8,512,64]{1,2,0:T(8,128)(2,1)},...) while((s32[]{:T(128)}, f32[8,64,64]{2,1,0:T(8,128)}, ...), condition=%wide.region_17.18_spmd.clone, body=%wide.region_14.0_spmd.clone.sunk | while | flops 8650690 | bytes 578401 | solution.py:105
  212.8 2.0 copy.220
  217.5 22.3 %while.81 = (s32[]{:T(128)}, f32[8,32,64]{2,1,0:T(8,128)S(1)}, f32[8,32]{1,0:T(8,128)}, bf16[8,32,64]{2,1,0:T(8,128)(2,1)}, bf16[8,512,64]{1,2,0:T(8,128)(2,1)},...) while((s32[]{:T(128)}, f32[8,32,64]{2,1,0:T(8,128)S(1)}, ...), condition=%wide.region_24.25_spmd.clone, body=%wide.region_21.24_spmd.clone.sunk | while | flops 4325346 | bytes 356449 | solution.py:105
  219.0 1.3 dynamic_update_slice.85
  221.8 1.3 dynamic_update_slice.85
  224.6 1.3 dynamic_update_slice.85
  242.5 2.0 copy.228
  247.2 12.3 %while.82 = (s32[]{:T(128)}, f32[8,16,64]{2,1,0:T(8,128)S(1)}, f32[8,16]{1,0:T(8,128)S(1)}, bf16[8,16,64]{2,1,0:T(8,128)(2,1)}, bf16[8,512,64]{1,2,0:T(8,128)(2,...) while((s32[]{:T(128)}, f32[8,16,64]{2,1,0:T(8,128)S(1)}, ...), condition=%wide.region_31.32_spmd.clone, body=%wide.region_28.31_spmd.clone.sunk | while | flops 2162674 | bytes 244897 | solution.py:105
  260.9 2.0 copy.237
  266.2 12.2 %while.83 = (s32[]{:T(128)}, f32[8,8,64]{2,1,0:T(8,128)S(1)}, f32[8,8]{1,0:T(8,128)S(1)}, bf16[8,8,64]{2,1,0:T(8,128)(2,1)}, bf16[8,512,64]{1,2,0:T(8,128)(2,1)}...) while((s32[]{:T(128)}, f32[8,8,64]{2,1,0:T(8,128)S(1)}, ...), condition=%wide.region_38.39_spmd.clone, body=%wide.region_35.38_spmd.clone.sunk | while | flops 1081338 | bytes 189313 | solution.py:105
  279.9 2.1 copy.246
  283.4 1.8 fusion.79
  285.2 1.5 fusion.144
  286.8 28.5 %reduce-scatter.3.cloned.1.call-done = f32[256,512]{1,0:T(8,128)} async-done(((f32[256,1024]{1,0:T(8,128)}), f32[256,512]{1,0:T(8,128)}) %reduce-scatter.3.cloned.1.call-update) | async-done | bytes 524304 | tf_op jit(solution)/shard_map/reduce_scatter | solution.py:135
  316.6 3.8 %psum.7 = f32[256]{0:T(256)S(1)} all-reduce(f32[256]{0:T(256)S(1)} %multiply_reduce_fusion), channel_id=1, replica_groups=mesh['seq'=128,'tp'=2] {'tp'}, use_global_device_ids=true, to_apply=%region_41.42 | all-reduce | flops 256 | bytes 2048 | tf_op jit(solution)/shard_map/psum | solution.py:138
  321.5 6.6 %all_gather.3 = bf16[256,1024]{1,0:T(8,128)(2,1)S(1)} all-gather(bf16[256,512]{1,0:T(8,128)(2,1)S(1)} %multiply_convert_fusion), channel_id=1, replica_groups=mesh['seq'=128,'tp'=2] {'tp'}, dimensions={1}, use_global_device_ids=true | all-gather | bytes 786432 | tf_op jit(solution)/shard_map/all_gather | solution.py:142
  328.2 1.7 fusion.145
  329.9 4.8 %convolution_convert_fusion = bf16[256,1024]{1,0:T(8,128)(2,1)} fusion(bf16[1024,1024]{1,0:T(8,128)(2,1)} %param.31, bf16[256,1024]{1,0:T(8,128)(2,1)S(1)} %all_gather.3, bf16[1024,1024]{1,0:T(8,128)(2,1)} %param.30, f32[256,1024]{1,0:T(8,128)} %fusion.145), kind=kOutput, calls=%fused_computation.109 | convolution fusion | flops 1075576832 | bytes 6291456 | tf_op jit(solution)/shard_map/dot_general | solution.py:147
  334.7 22.8 %reduce-scatter.5.cloned.1.call-done = bf16[256,512]{1,0:T(8,128)(2,1)} async-done(((bf16[256,1024]{1,0:T(8,128)(2,1)}), bf16[256,512]{1,0:T(8,128)(2,1)}) %reduce-scatter.5.cloned.1.call-update) | async-done | bytes 262160 | tf_op jit(solution)/shard_map/reduce_scatter | solution.py:146
  357.5 1.8 add_convert_fusion
  (563 shorter events, 182.7 us)
Async XLA Ops:
  6.5 321.6 %copy-start = (bf16[1024,1024]{1,0:T(8,128)(2,1)S(1)}, bf16[1024,1024]{1,0:T(8,128)(2,1)}, u32[]{:S(2)}) copy-start(bf16[1024,1024]{1,0:T(8,128)(2,1)} %param.29) | copy-start | bytes 6291460
  6.5 308.8 %reduce-scatter.3.cloned.1.call-start = ((), (), s32[]{:S(2)}) async-start(), calls=%async_computation.2 | async-start | bytes 1572864 | tf_op jit(solution)/shard_map/reduce_scatter | solution.py:135
  11.9 11.3 %copy-start.3 = (bf16[256,512]{1,0:T(8,128)(2,1)S(1)}, bf16[256,512]{1,0:T(8,128)(2,1)}, u32[]{:S(2)}) copy-start(bf16[256,512]{1,0:T(8,128)(2,1)} %param.23) | copy-start | bytes 786436
  14.0 9.5 %copy-start.1 = (bf16[256,512]{1,0:T(8,128)(2,1)S(1)}, bf16[256,512]{1,0:T(8,128)(2,1)}, u32[]{:S(2)}) copy-start(bf16[256,512]{1,0:T(8,128)(2,1)} %param.24) | copy-start | bytes 786436
  14.0 10.5 %copy-start.2 = (bf16[256,512]{1,0:T(8,128)(2,1)S(1)}, bf16[256,512]{1,0:T(8,128)(2,1)}, u32[]{:S(2)}) copy-start(bf16[256,512]{1,0:T(8,128)(2,1)} %param.25) | copy-start | bytes 786436
  20.0 79.1 %collective-permute-start.1 = (bf16[1,128,1024]{1,2,0:T(8,128)(2,1)}, bf16[1,128,1024]{1,2,0:T(8,128)(2,1)}, u32[]{:S(2)}, u32[]{:S(2)}) collective-permute-start(bf16[1,128,1024]{1,2,0:T(8,128)(2,1)} %maximum_bitcast_fusion.2), channel_id=1, source_target_pairs={{0,2},{2,0},{4,6},{6,4},{8,10},{10,8},{12,14},{14,12},{16,18},{18,... | collective-permute-start | bytes 786440 | tf_op jit(solution)/shard_map/ppermute | solution.py:21
  31.8 59.9 %collective-permute-start.3 = (bf16[1,64,1024]{2,1,0:T(8,128)(2,1)}, bf16[1,64,1024]{2,1,0:T(8,128)(2,1)}, u32[]{:S(2)}, u32[]{:S(2)}) collective-permute-start(bf16[1,64,1024]{2,1,0:T(8,128)(2,1)} %maximum_bitcast_fusion.3), channel_id=1, source_target_pairs={{0,2},{2,0},{4,6},{6,4},{8,10},{10,8},{12,14},{14,12},{16,18},{18,... | collective-permute-start | bytes 393224 | tf_op jit(solution)/shard_map/ppermute | solution.py:21
  40.0 44.5 %collective-permute-start.6 = (bf16[1,32,1024]{2,1,0:T(8,128)(2,1)}, bf16[1,32,1024]{2,1,0:T(8,128)(2,1)}, u32[]{:S(2)}, u32[]{:S(2)}) collective-permute-start(bf16[1,32,1024]{2,1,0:T(8,128)(2,1)} %maximum_bitcast_fusion.4), channel_id=1, source_target_pairs={{0,2},{2,0},{4,6},{6,4},{8,10},{10,8},{12,14},{14,12},{16,18},{18,... | collective-permute-start | bytes 196616 | tf_op jit(solution)/shard_map/ppermute | solution.py:21
  48.2 33.4 %collective-permute-start.10 = (bf16[1,16,1024]{2,1,0:T(8,128)(2,1)}, bf16[1,16,1024]{2,1,0:T(8,128)(2,1)}, u32[]{:S(2)}, u32[]{:S(2)}) collective-permute-start(bf16[1,16,1024]{2,1,0:T(8,128)(2,1)} %maximum_bitcast_fusion.5), channel_id=1, source_target_pairs={{0,2},{2,0},{4,6},{6,4},{8,10},{10,8},{12,14},{14,12},{16,18},{18,... | collective-permute-start | bytes 98312 | tf_op jit(solution)/shard_map/ppermute | solution.py:21
  54.2 7.9 %copy-start.19 = (bf16[128,8,64]{2,1,0:T(8,128)(2,1)S(1)}, bf16[128,8,64]{2,1,0:T(8,128)(2,1)}, u32[]{:S(2)}) copy-start(bf16[128,8,64]{2,1,0:T(8,128)(2,1)} %get-tuple-element.529) | copy-start | bytes 393220
  54.2 8.7 %copy-start.25 = (bf16[64,8,64]{2,1,0:T(8,128)(2,1)S(1)}, bf16[64,8,64]{2,1,0:T(8,128)(2,1)}, u32[]{:S(2)}) copy-start(bf16[64,8,64]{2,1,0:T(8,128)(2,1)} %get-tuple-element.526) | copy-start | bytes 196612
  54.2 9.3 %copy-start.30 = (bf16[32,8,64]{2,1,0:T(8,128)(2,1)S(1)}, bf16[32,8,64]{2,1,0:T(8,128)(2,1)}, u32[]{:S(2)}) copy-start(bf16[32,8,64]{2,1,0:T(8,128)(2,1)} %get-tuple-element.523) | copy-start | bytes 98308
  56.5 24.3 %collective-permute-start.15 = (bf16[1,8,1024]{2,1,0:T(8,128)(2,1)}, bf16[1,8,1024]{2,1,0:T(8,128)(2,1)}, u32[]{:S(2)}, u32[]{:S(2)}) collective-permute-start(bf16[1,8,1024]{2,1,0:T(8,128)(2,1)} %maximum_bitcast_fusion.6), channel_id=1, source_target_pairs={{0,2},{2,0},{4,6},{6,4},{8,10},{10,8},{12,14},{14,12},{16,18},{18,... | collective-permute-start | bytes 49160 | tf_op jit(solution)/shard_map/ppermute | solution.py:21
  57.8 28.9 %copy-start.27 = (bf16[32,512]{1,0:T(8,128)(2,1)S(1)}, bf16[32,512]{1,0:T(8,128)(2,1)}, u32[]{:S(2)}) copy-start(bf16[32,512]{1,0:T(8,128)(2,1)} %copy-done.26) | copy-start | bytes 98308
  57.8 28.9 %copy-start.29 = (bf16[32,512]{1,0:T(8,128)(2,1)S(1)}, bf16[32,512]{1,0:T(8,128)(2,1)}, u32[]{:S(2)}) copy-start(bf16[32,512]{1,0:T(8,128)(2,1)} %copy-done.28) | copy-start | bytes 98308
  62.8 18.8 %copy-start.32 = (bf16[16,512]{1,0:T(8,128)(2,1)S(1)}, bf16[16,512]{1,0:T(8,128)(2,1)}, u32[]{:S(2)}) copy-start(bf16[16,512]{1,0:T(8,128)(2,1)} %copy-done.31) | copy-start | bytes 49156
  62.8 30.3 %copy-start.22 = (bf16[64,512]{1,0:T(8,128)(2,1)S(1)}, bf16[64,512]{1,0:T(8,128)(2,1)}, u32[]{:S(2)}) copy-start(bf16[64,512]{1,0:T(8,128)(2,1)} %copy-done.21) | copy-start | bytes 196612
  62.9 30.3 %copy-start.24 = (bf16[64,512]{1,0:T(8,128)(2,1)S(1)}, bf16[64,512]{1,0:T(8,128)(2,1)}, u32[]{:S(2)}) copy-start(bf16[64,512]{1,0:T(8,128)(2,1)} %copy-done.23) | copy-start | bytes 196612
  80.8 33.6 %collective-permute-start = (bf16[1,256,1024]{2,1,0:T(8,128)(2,1)}, bf16[1,256,1024]{2,1,0:T(8,128)(2,1)S(1)}, u32[]{:S(2)}, u32[]{:S(2)}) collective-permute-start(bf16[1,256,1024]{2,1,0:T(8,128)(2,1)} %maximum_bitcast_fusion.1), channel_id=1, source_target_pairs={{0,2},{2,0},{4,6},{6,4},{8,10},{10,8},{12,14},{14,12},{16,18},{18,... | collective-permute-start | bytes 1572872 | tf_op jit(solution)/shard_map/ppermute | solution.py:21
  81.6 2.9 collective-permute-start.16
  84.4 3.2 collective-permute-start.11
  84.5 4.7 %collective-permute-start.17 = (bf16[4,8,1024]{2,1,0:T(8,128)(2,1)S(1)}, bf16[4,8,1024]{2,1,0:T(8,128)(2,1)S(1)}, u32[]{:S(2)}, u32[]{:S(2)}) collective-permute-start(bf16[4,8,1024]{2,1,0:T(8,128)(2,1)S(1)} %pad_maximum_fusion.18), channel_id=1, source_target_pairs={{0,8},{8,0},{2,10},{10,2},{4,12},{12,4},{6,14},{14,6},{16,24},{24,... | collective-permute-start | bytes 196616 | tf_op jit(solution)/shard_map/ppermute | solution.py:21
  87.6 6.6 %collective-permute-start.7 = (bf16[2,32,1024]{2,1,0:T(8,128)(2,1)S(1)}, bf16[2,32,1024]{2,1,0:T(8,128)(2,1)S(1)}, u32[]{:S(2)}, u32[]{:S(2)}) collective-permute-start(bf16[2,32,1024]{2,1,0:T(8,128)(2,1)S(1)} %pad_maximum_fusion.14), channel_id=1, source_target_pairs={{0,4},{4,0},{2,6},{6,2},{8,12},{12,8},{10,14},{14,10},{16,20},{20,... | collective-permute-start | bytes 393224 | tf_op jit(solution)/shard_map/ppermute | solution.py:21
  89.2 5.6 %collective-permute-start.12 = (bf16[4,16,1024]{2,1,0:T(8,128)(2,1)S(1)}, bf16[4,16,1024]{2,1,0:T(8,128)(2,1)S(1)}, u32[]{:S(2)}, u32[]{:S(2)}) collective-permute-start(bf16[4,16,1024]{2,1,0:T(8,128)(2,1)S(1)} %pad_maximum_fusion.15), channel_id=1, source_target_pairs={{0,8},{8,0},{2,10},{10,2},{4,12},{12,4},{6,14},{14,6},{16,24},{24,... | collective-permute-start | bytes 393224 | tf_op jit(solution)/shard_map/ppermute | solution.py:21
  91.6 10.5 %copy-start.18 = (bf16[128,8,64]{0,2,1:T(8,128)(2,1)S(1)}, bf16[128,8,64]{0,2,1:T(8,128)(2,1)}, u32[]{:S(2)}) copy-start(bf16[128,8,64]{0,2,1:T(8,128)(2,1)} %copy-done.17) | copy-start | bytes 393220
  91.6 6.0 %collective-permute-start.18 = (bf16[8,8,1024]{2,1,0:T(8,128)(2,1)S(1)}, bf16[8,8,1024]{2,1,0:T(8,128)(2,1)S(1)}, u32[]{:S(2)}, u32[]{:S(2)}) collective-permute-start(bf16[8,8,1024]{2,1,0:T(8,128)(2,1)S(1)} %pad_maximum_fusion.16), channel_id=1, source_target_pairs={{0,16},{16,0},{2,18},{18,2},{4,20},{20,4},{6,22},{22,6},{8,24},{24... | collective-permute-start | bytes 393224 | tf_op jit(solution)/shard_map/ppermute | solution.py:21
  94.2 9.9 %collective-permute-start.4 = (bf16[2,64,1024]{2,1,0:T(8,128)(2,1)S(1)}, bf16[2,64,1024]{2,1,0:T(8,128)(2,1)S(1)}, u32[]{:S(2)}, u32[]{:S(2)}) collective-permute-start(bf16[2,64,1024]{2,1,0:T(8,128)(2,1)S(1)} %pad_maximum_fusion.10), channel_id=1, source_target_pairs={{0,4},{4,0},{2,6},{6,2},{8,12},{12,8},{10,14},{14,10},{16,20},{20,... | collective-permute-start | bytes 786440 | tf_op jit(solution)/shard_map/ppermute | solution.py:21
  94.8 11.2 %collective-permute-start.8 = (bf16[4,32,1024]{2,1,0:T(8,128)(2,1)S(1)}, bf16[4,32,1024]{2,1,0:T(8,128)(2,1)S(1)}, u32[]{:S(2)}, u32[]{:S(2)}) collective-permute-start(bf16[4,32,1024]{2,1,0:T(8,128)(2,1)S(1)} %pad_maximum_fusion.11), channel_id=1, source_target_pairs={{0,8},{8,0},{2,10},{10,2},{4,12},{12,4},{6,14},{14,6},{16,24},{24,... | collective-permute-start | bytes 786440 | tf_op jit(solution)/shard_map/ppermute | solution.py:21
  97.6 11.5 %collective-permute-start.13 = (bf16[8,16,1024]{2,1,0:T(8,128)(2,1)S(1)}, bf16[8,16,1024]{2,1,0:T(8,128)(2,1)S(1)}, u32[]{:S(2)}, u32[]{:S(2)}) collective-permute-start(bf16[8,16,1024]{2,1,0:T(8,128)(2,1)S(1)} %pad_maximum_fusion.12), channel_id=1, source_target_pairs={{0,16},{16,0},{2,18},{18,2},{4,20},{20,4},{6,22},{22,6},{8,24},{24... | collective-permute-start | bytes 786440 | tf_op jit(solution)/shard_map/ppermute | solution.py:21
  99.1 11.6 %collective-permute-start.19 = (bf16[16,8,1024]{2,1,0:T(8,128)(2,1)S(1)}, bf16[16,8,1024]{2,1,0:T(8,128)(2,1)S(1)}, u32[]{:S(2)}, u32[]{:S(2)}) collective-permute-start(bf16[16,8,1024]{2,1,0:T(8,128)(2,1)S(1)} %pad_maximum_fusion.13), channel_id=1, source_target_pairs={{0,32},{32,0},{2,34},{34,2},{4,36},{36,4},{6,38},{38,6},{8,40},{40... | collective-permute-start | bytes 786440 | tf_op jit(solution)/shard_map/ppermute | solution.py:21
  103.2 5.0 %copy-start.13 = (bf16[1,128,1024]{1,2,0:T(8,128)(2,1)}, bf16[1,128,1024]{1,2,0:T(8,128)(2,1)S(1)}, u32[]{:S(2)}) copy-start(bf16[1,128,1024]{1,2,0:T(8,128)(2,1)S(1)} %get-tuple-element.664) | copy-start | bytes 786436
  104.1 55.3 %collective-permute-start.2 = (bf16[2,128,1024]{1,2,0:T(8,128)(2,1)}, bf16[2,128,1024]{1,2,0:T(8,128)(2,1)}, u32[]{:S(2)}, u32[]{:S(2)}) collective-permute-start(bf16[2,128,1024]{1,2,0:T(8,128)(2,1)} %pad_maximum_fusion.5), channel_id=1, source_target_pairs={{0,4},{4,0},{2,6},{6,2},{8,12},{12,8},{10,14},{14,10},{16,20},{20,... | collective-permute-start | bytes 1572872 | tf_op jit(solution)/shard_map/ppermute | solution.py:21
  106.0 84.1 %collective-permute-start.5 = (bf16[4,64,1024]{2,1,0:T(8,128)(2,1)}, bf16[4,64,1024]{2,1,0:T(8,128)(2,1)}, u32[]{:S(2)}, u32[]{:S(2)}) collective-permute-start(bf16[4,64,1024]{2,1,0:T(8,128)(2,1)} %pad_maximum_fusion.6), channel_id=1, source_target_pairs={{0,8},{8,0},{2,10},{10,2},{4,12},{12,4},{6,14},{14,6},{16,24},{24,... | collective-permute-start | bytes 1572872 | tf_op jit(solution)/shard_map/ppermute | solution.py:21
  109.2 105.6 %collective-permute-start.9 = (bf16[8,32,1024]{2,1,0:T(8,128)(2,1)}, bf16[8,32,1024]{2,1,0:T(8,128)(2,1)}, u32[]{:S(2)}, u32[]{:S(2)}) collective-permute-start(bf16[8,32,1024]{2,1,0:T(8,128)(2,1)} %pad_maximum_fusion.7), channel_id=1, source_target_pairs={{0,16},{16,0},{2,18},{18,2},{4,20},{20,4},{6,22},{22,6},{8,24},{24... | collective-permute-start | bytes 1572872 | tf_op jit(solution)/shard_map/ppermute | solution.py:21
  109.8 3.7 %copy-start.8 = (bf16[8,16,1024]{2,1,0:T(8,128)(2,1)}, bf16[8,16,1024]{2,1,0:T(8,128)(2,1)S(1)}, u32[]{:S(2)}) copy-start(bf16[8,16,1024]{2,1,0:T(8,128)(2,1)S(1)} %get-tuple-element.670) | copy-start | bytes 786436
  110.7 133.8 %collective-permute-start.14 = (bf16[16,16,1024]{2,1,0:T(8,128)(2,1)}, bf16[16,16,1024]{2,1,0:T(8,128)(2,1)}, u32[]{:S(2)}, u32[]{:S(2)}) collective-permute-start(bf16[16,16,1024]{2,1,0:T(8,128)(2,1)} %pad_maximum_fusion.8), channel_id=1, source_target_pairs={{0,32},{32,0},{2,34},{34,2},{4,36},{36,4},{6,38},{38,6},{8,40},{40... | collective-permute-start | bytes 1572872 | tf_op jit(solution)/shard_map/ppermute | solution.py:21
  113.5 9.9 %copy-start.6 = (bf16[16,8,1024]{2,1,0:T(8,128)(2,1)}, bf16[16,8,1024]{2,1,0:T(8,128)(2,1)S(1)}, u32[]{:S(2)}) copy-start(bf16[16,8,1024]{2,1,0:T(8,128)(2,1)S(1)} %get-tuple-element.672) | copy-start | bytes 786436
  114.4 149.2 %collective-permute-start.20 = (bf16[32,8,1024]{2,1,0:T(8,128)(2,1)}, bf16[32,8,1024]{2,1,0:T(8,128)(2,1)}, u32[]{:S(2)}, u32[]{:S(2)}) collective-permute-start(bf16[32,8,1024]{2,1,0:T(8,128)(2,1)} %pad_maximum_fusion.9), channel_id=1, source_target_pairs={{0,64},{64,0},{2,66},{66,2},{4,68},{68,4},{6,70},{70,6},{8,72},{72... | collective-permute-start | bytes 1572872 | tf_op jit(solution)/shard_map/ppermute | solution.py:21
  119.5 3.9 %copy-start.65 = (s32[256]{0:T(256)S(1)}, s32[256]{0:T(256)}, u32[]{:S(2)}) copy-start(s32[256]{0:T(256)} %iota_add_fusion) | copy-start | bytes 3076
  123.4 36.0 %copy-start.14 = (bf16[1,128,1024]{1,2,0:T(8,128)(2,1)S(1)}, bf16[1,128,1024]{1,2,0:T(8,128)(2,1)}, u32[]{:S(2)}) copy-start(bf16[1,128,1024]{1,2,0:T(8,128)(2,1)} %copy-done.13) | copy-start | bytes 786436
  163.1 3.6 copy-start.63
  163.1 3.6 copy-start.66
  259.5 3.4 copy-start.36
  259.5 3.4 copy-start.44
  259.5 3.4 copy-start.48
  259.5 3.4 copy-start.50
  278.4 3.6 copy-start.45
  278.5 3.6 copy-start.46
  278.5 3.6 copy-start.47
  278.5 3.6 copy-start.49
  278.5 3.6 copy-start.51
  278.5 3.6 copy-start.53
  278.5 3.6 copy-start.55
  278.5 3.6 copy-start.59
  278.8 4.6 %copy-start.38 = (f32[256,8]{0,1:T(8,128)S(1)}, f32[256,8]{0,1:T(8,128)}, u32[]{:S(2)}) copy-start(f32[256,8]{0,1:T(8,128)} %mul.481) | copy-start | bytes 24580
  278.8 4.6 %copy-start.39 = (f32[256,8]{0,1:T(8,128)S(1)}, f32[256,8]{0,1:T(8,128)}, u32[]{:S(2)}) copy-start(f32[256,8]{0,1:T(8,128)} %copy.219) | copy-start | bytes 24580
  278.8 4.6 %copy-start.40 = (f32[256,8]{0,1:T(8,128)S(1)}, f32[256,8]{0,1:T(8,128)}, u32[]{:S(2)}) copy-start(f32[256,8]{0,1:T(8,128)} %copy.205) | copy-start | bytes 24580
  278.8 4.6 %copy-start.41 = (f32[256,8]{0,1:T(8,128)S(1)}, f32[256,8]{0,1:T(8,128)}, u32[]{:S(2)}) copy-start(f32[256,8]{0,1:T(8,128)} %mul.499) | copy-start | bytes 24580
  278.8 4.6 %copy-start.42 = (f32[256,8]{0,1:T(8,128)S(1)}, f32[256,8]{0,1:T(8,128)}, u32[]{:S(2)}) copy-start(f32[256,8]{0,1:T(8,128)} %mul.517) | copy-start | bytes 24580
  279.9 3.5 copy-start.15
  279.9 3.5 copy-start.16
  285.2 30.2 %copy-start.5 = (bf16[256,512]{1,0:T(8,128)(2,1)S(1)}, bf16[256,512]{1,0:T(8,128)(2,1)}, u32[]{:S(2)}) copy-start(bf16[256,512]{1,0:T(8,128)(2,1)} %param.22) | copy-start | bytes 786436
  286.7 70.8 %reduce-scatter.5.cloned.1.call-start = ((), (), s32[]{:S(2)}) async-start(), calls=%async_computation.3 | async-start | bytes 786432 | tf_op jit(solution)/shard_map/reduce_scatter | solution.py:146
  329.9 27.6 %copy-start.4 = (f32[256,512]{1,0:T(8,128)S(1)}, f32[256,512]{1,0:T(8,128)}, u32[]{:S(2)}) copy-start(f32[256,512]{1,0:T(8,128)} %reduce-scatter.3.cloned.1.call-done) | copy-start | bytes 1572868
  (26 other events, 37.5 us)
Sparse Core Ops, SparseCore 0:
  286.8 28.5 reduce-scatter.2
  334.8 22.6 reduce-scatter.4
where the time goes:
time: 372 us; the launch traced here: 366 us
  local copies, waits for them, and re-layouts  103 us (28%)
  matrix products  92.9 us (25%)
  other arithmetic  60.5 us (16%)
  waiting for transfers between devices  55 us (15%)
  starting transfers between devices  29.2 us (8%)
  between operations  14.7 us (4%)
  blocking collectives  10.4 us (3%)
    dot_general x48, matrix products, attend(): jnp.dot(query, key_block.T, preferred_element_type=jnp.float32) * scale  52.5 us
    dot_general x48, matrix products, attend(): output = jnp.dot(weights, value_block, preferred_element_type=jnp.float32)  32.5 us
    ppermute x21, starting transfers between devices, from_partner(): return lax.ppermute(block, axis, route)  29.1 us
    reduce_scatter x1, waiting for transfers between devices, shards(): lax.psum_scatter(partial_value, 'tp', scatter_dimension=1, tiled=True)  28.5 us
    reduce_scatter x1, waiting for transfers between devices, shards(): lax.psum_scatter(jnp.dot(act, down_weight, preferred_element_type=jnp.flo...  22.8 us
    mul x25, local copies, waits for them, and re-layouts, shards(): outputs.transpose(1, 0, 2)[:, None] * chosen[None, :, :, None]  22.4 us
    dynamic_update_slice x48, local copies, waits for them, and re-layouts, shards(): outputs, logs = lax.map(attend, (query_rows, key_rows, value_rows))  21.5 us
    another operation x15, local copies, waits for them, and re-layouts, pick_rows(): shaped = array.reshape(count, rate, array.shape[1], array.shape[2])  15.1 us
  transfers between devices with their start and end apart: 23, of which 5 were waited for; matrix products, arithmetic and copies ran while one was open for 57% of the time, Pallas kernels for 0%

commit v1 on v0

v1 whole, which is shorter than its diff:
```python
import math

import jax
import jax.numpy as jnp
from jax import lax
from jax.experimental import pallas as pl
from jax.experimental.pallas import tpu as pltpu
from jax.sharding import PartitionSpec as P

MESH = pl.DeviceIdType.MESH
F32 = jnp.float32
BF16 = jnp.bfloat16

ROWS = 256
COLS = 512
GROUP = 8
ZED = 8
MASKED = -1e30
EXPONENT = math.log2(math.e) / 8.0


def lanes(shape):
    return lax.broadcasted_iota(jnp.int32, shape, len(shape) - 1)


def sublanes(shape):
    return lax.broadcasted_iota(jnp.int32, shape, 0)


def swap(x):
    return pltpu.roll(x, 64, 1)


def mm(a, b):
    return lax.dot_general(a, b, (((1,), (0,)), ((), ())), preferred_element_type=F32)


def mmt(a, b):
    return lax.dot_general(a, b, (((1,), (1,)), ((), ())), preferred_element_type=F32)


def with_ones(kv):
    lane = lanes(kv.shape)
    return jnp.where(lane < 64, jnp.where(lane == 0, 1.0, 0.0), kv.astype(F32)).astype(BF16)


def branch_of(i):
    one = jnp.where(i < 192, 2, jnp.where(i < 224, 3, jnp.where(i < 240, 4, jnp.where(i < 248, 5, 6))))
    return jnp.where(i < 128, 1, one)


def layer(
    queries,
    keys,
    values,
    residual,
    out_weight,
    gain,
    offsets,
    gate_hbm,
    up_hbm,
    down_hbm,
    out,
    send,
    got,
    pick_kv,
    pick_v1,
    pick_q,
    far_q,
    k3,
    k4,
    k5,
    near_out,
    pick_out,
    choose,
    choose_t,
    mix_send,
    mix_own,
    mix_far,
    mix_wide,
    res_all,
    out_far,
    gate_w,
    up_w,
    down_w,
    hidden,
    normed,
    act,
    down_send,
    down_got,
    a_send,
    a_got,
    z_send,
    z_got,
    m_send,
    m_got,
    f_send,
    f_got,
    w_send,
    w_got,
    r_send,
    r_got,
    d_send,
    d_got,
    local,
):
    seq = lax.axis_index("seq")
    tp = lax.axis_index("tp")
    base = (seq // GROUP) * GROUP
    me = seq % GROUP
    y = me // 2
    core = me % 2
    z = (seq // GROUP) % ZED
    half = seq // (GROUP * ZED)
    plane = half * (GROUP * ZED)
    partner = (seq, 1 - tp)
    behind = ((1 - half) * (GROUP * ZED) + seq % (GROUP * ZED), 1 - tp)
    sibling = (base + me + 1 - 2 * core, tp)

    def remote(src, dst, s, r, to):
        return pltpu.make_async_remote_copy(
            src_ref=src, dst_ref=dst, send_sem=s, recv_sem=r, device_id=to, device_id_type=MESH
        )

    loads = [
        pltpu.make_async_copy(gate_hbm, gate_w, local.at[0]),
        pltpu.make_async_copy(up_hbm, up_w, local.at[1]),
        pltpu.make_async_copy(down_hbm, down_w, local.at[2]),
    ]

    k3[...] = jnp.zeros_like(k3)
    k4[...] = jnp.zeros_like(k4)
    k5[...] = jnp.zeros_like(k5)
    barrier = pltpu.get_barrier_semaphore()
    for k in range(1, GROUP):
        pl.semaphore_signal(barrier, inc=1, device_id=(base + (me + k) % GROUP, tp), device_id_type=MESH)
    for d in range(1, ZED):
        pl.semaphore_signal(
            barrier, inc=1, device_id=(plane + ((z + d) % ZED) * GROUP + me, tp), device_id_type=MESH
        )
    pl.semaphore_signal(barrier, inc=1, device_id=partner, device_id_type=MESH)
    pl.semaphore_signal(barrier, inc=1, device_id=behind, device_id_type=MESH)

    low = lanes((ROWS, 128)) < 64
    low_half = lanes((128, 128)) < 64
    for pair in range(GROUP // 2):
        cut = slice(128 * pair, 128 * pair + 128)
        k = keys[:, cut].astype(F32)
        v = values[:, cut].astype(F32)
        q = queries[:, cut].astype(F32)
        send[2 * pair, 0:ROWS] = jnp.where(low, k, swap(v)).astype(BF16)
        send[2 * pair + 1, 0:ROWS] = jnp.where(low, swap(k), v).astype(BF16)
        top, bottom = q[0:128], q[128:256]
        send[2 * pair, ROWS : ROWS + 128] = jnp.where(low_half, top, swap(bottom)).astype(BF16)
        send[2 * pair + 1, ROWS : ROWS + 128] = jnp.where(low_half, swap(top), bottom).astype(BF16)

    pl.semaphore_wait(barrier, 2 * (GROUP - 1) + 2)

    def block_copy(to):
        return remote(send.at[to], got.at[me], a_send.at[to], a_got.at[me], (base + to, tp))

    a_out = []
    for step in (2, 1, 3):
        for c in range(2):
            a_out.append(block_copy(((y + step) % 4) * 2 + c))
            a_out[-1].start()
    a_out.append(block_copy(me + 1 - 2 * core))
    a_out[-1].start()
    got[me] = send[me]

    w_first = core * 128
    w_second = 256 + core * 128

    def w_piece(first, i, to, src):
        piece = pl.ds(pl.multiple_of(first, 128), 128)
        return remote(src.at[piece], out_far.at[piece], w_send.at[i], w_got.at[i], to)

    w_out = [w_piece(w_first, 0, partner, out_weight), w_piece(w_second, 1, behind, out_weight)]
    res_copy = remote(residual, res_all.at[tp], r_send, r_got, partner)
    res_copy.start()
    for copy in w_out:
        copy.start()
    for load in loads:
        load.start()
    res_all[tp] = residual[...]

    def target(i):
        spot = jnp.full(i.shape, -1, jnp.int32)
        first = 0
        for b in range(1, 6):
            rate = 2**b
            count = ROWS // rate
            off = offsets[b, me] & (rate - 1)
            inside = (i >= first) & (i < first + count)
            spot = jnp.where(inside, (i - first) * rate + off, spot)
            first += count
        return spot

    square = (ROWS, ROWS)
    choose[...] = jnp.where(lanes(square) == target(sublanes(square)), 1.0, 0.0).astype(BF16)
    choose_t[...] = jnp.where(sublanes(square) == target(lanes(square)), 1.0, 0.0).astype(BF16)
    pick_out[:, 248:256] = jnp.zeros((GROUP, 8, 128), F32)

    z3 = z % 2
    z4 = z % 4

    def z_copy(which, d, sender, to):
        buffer, count, slot, at = (
            (k3, 256, sender % 2, 0),
            (k4, 128, sender % 4, d),
            (k5, 64, sender, 3 + d),
        )[which]
        piece = buffer.at[pl.ds(pl.multiple_of(slot * count, 64), count)]
        return remote(piece, piece, z_send.at[at], z_got.at[at], (plane + to * GROUP + me, tp))

    def z_each(act_on):
        for d in range(ZED - 1, 0, -1):
            if d == 1:
                act_on(0, d, z3)
            if d < 4:
                act_on(1, d, z4)
            act_on(2, d, z)

    def z_start():
        sizes = (2, 4, 8)

        def one(which, d, slot):
            @pl.when(slot + d < sizes[which])
            def _():
                z_copy(which, d, z, (z + d) % ZED).start()

        z_each(one)

    def z_finish_send():
        sizes = (2, 4, 8)

        def one(which, d, slot):
            @pl.when(slot + d < sizes[which])
            def _():
                z_copy(which, d, z, (z + d) % ZED).wait_send()

        z_each(one)

    def z_finish_got():
        def one(which, d, slot):
            @pl.when(slot >= d)
            def _():
                z_copy(which, d, (z + ZED - d) % ZED, z).wait_recv()

        z_each(one)

    def finish(o, top):
        return o + jnp.where(lanes(o.shape) == 1, top, 0.0)

    tri = lanes(square) <= sublanes(square)

    def causal_pair(q0, q1, kv0, kv1, v0, v1):
        s00 = jnp.where(tri, mmt(q0, kv0), MASKED)
        s10 = mmt(q1, kv0)
        s11 = jnp.where(tri, mmt(q1, kv1), MASKED)
        t0 = jnp.max(s00, axis=1, keepdims=True)
        t1 = jnp.max(jnp.maximum(s10, s11), axis=1, keepdims=True)
        p00 = jnp.exp2((s00 - t0) * EXPONENT).astype(BF16)
        p10 = jnp.exp2((s10 - t1) * EXPONENT).astype(BF16)
        p11 = jnp.exp2((s11 - t1) * EXPONENT).astype(BF16)
        return finish(mm(p00, v0), t0), finish(mm(p10, v0) + mm(p11, v1), t1)

    def near(m, carry):
        j = (y + m + (m // 2) * (5 - 2 * m)) % 4

        def wait(s):
            remote(send.at[s], got.at[s], a_send.at[s], a_got.at[s], (base + s, tp)).wait_recv()

        wait_core = jnp.where(m == 0, 1 - core, 1)

        @pl.when(m > 0)
        def _():
            wait(2 * j)

        wait(2 * j + wait_core)
        kvs, qs, v1s, parts = [], [], [], []
        for i in range(2):
            kv = got[2 * j + i, 0:ROWS]
            packed = got[2 * j + i, ROWS : ROWS + 128].astype(F32)
            q = jnp.concatenate(
                [jnp.where(low_half, packed, 0.0), jnp.where(low_half, swap(packed), 0.0)], axis=0
            ).astype(BF16)
            kvs.append(kv)
            qs.append(q)
            v1s.append(with_ones(kv))
            parts.append((mm(choose[...], kv), mm(choose[...], q)))
        for i in range(2):
            kv, q = parts[i]
            pick_kv[j, 128 * i : 128 * i + 128] = kv[0:128].astype(BF16)
            pick_v1[j, 128 * i : 128 * i + 128] = with_ones(kv[0:128])
            pick_q[j, 128 * i : 128 * i + 128] = q[0:128].astype(BF16)

        def both(which, first, last):
            return jnp.concatenate([parts[0][which][first:last], parts[1][which][first:last]], axis=0)

        at = pl.ds(pl.multiple_of((j % 2) * 128, 128), 128)
        pick_kv[4 + j // 2, at] = both(0, 128, 192).astype(BF16)
        pick_v1[4 + j // 2, at] = with_ones(both(0, 128, 192))
        pick_q[4 + j // 2, at] = both(1, 128, 192).astype(BF16)
        k3[pl.ds(pl.multiple_of(z3 * 256 + j * 64, 64), 64)] = both(0, 192, 224).astype(BF16)
        far_q[pl.ds(pl.multiple_of(j * 64, 64), 64)] = both(1, 192, 224).astype(BF16)
        k4[pl.ds(pl.multiple_of(z4 * 128 + j * 32, 32), 32)] = both(0, 224, 240).astype(BF16)
        far_q[pl.ds(pl.multiple_of(256 + j * 32, 32), 32)] = both(1, 224, 240).astype(BF16)
        k5[pl.ds(pl.multiple_of(z * 64 + j * 16, 16), 16)] = both(0, 240, 248).astype(BF16)
        far_q[pl.ds(pl.multiple_of(384 + j * 16, 16), 16)] = both(1, 240, 248).astype(BF16)

        @pl.when(m == 3)
        def _():
            z_start()

        o0, o1 = causal_pair(qs[0], qs[1], kvs[0], kvs[1], v1s[0], v1s[1])
        near_out[2 * j] = o0
        near_out[2 * j + 1] = o1
        return carry

    lax.fori_loop(0, 4, near, 0)

    for copy in w_out:
        copy.wait_recv()
    w_on = [w_piece(w_first, 2, sibling, out_far), w_piece(w_second, 3, sibling, out_far)]
    for copy in w_on:
        copy.start()

    def picked(i, carry):
        o0, o1 = causal_pair(
            pick_q[2 * i],
            pick_q[2 * i + 1],
            pick_kv[2 * i],
            pick_kv[2 * i + 1],
            pick_v1[2 * i],
            pick_v1[2 * i + 1],
        )

        @pl.when(i < 2)
        def _():
            pick_out[4 * i, 0:128] = o0[0:128]
            pick_out[4 * i + 1, 0:128] = o0[128:256]
            pick_out[4 * i + 2, 0:128] = o1[0:128]
            pick_out[4 * i + 3, 0:128] = o1[128:256]

        @pl.when(i == 2)
        def _():
            for u in range(4):
                pick_out[u, 128:192] = o0[64 * u : 64 * u + 64]
                pick_out[4 + u, 128:192] = o1[64 * u : 64 * u + 64]

        return carry

    lax.fori_loop(0, 3, picked, 0)

    z_finish_got()
    for buffer, q_first, count, slot, first in (
        (k3, 0, 256, z3, 192),
        (k4, 256, 128, z4, 224),
        (k5, 384, 64, z, 240),
    ):
        kv = buffer[...]
        q = far_q[q_first : q_first + count]
        shape = (count, 512)
        s = jnp.where(lanes(shape) <= sublanes(shape) + slot * count, mmt(q, kv), MASKED)
        t = jnp.max(s, axis=1, keepdims=True)
        p = jnp.exp2((s - t) * EXPONENT).astype(BF16)
        o = finish(mm(p, with_ones(kv)), t)
        each = count // GROUP
        for u in range(GROUP):
            pick_out[u, first : first + each] = o[each * u : each * u + each]

    tile = (ROWS, 128)
    lane = lanes(tile)
    mine = lane == branch_of(sublanes(tile))
    covered = jnp.zeros(tile, jnp.int32)
    for b in range(1, 6):
        off = offsets[b, me] & (2**b - 1)
        hit = jnp.where(sublanes(tile) % 2**b == off, 1, 0)
        covered = jnp.where(lane == b, hit, covered)

    def split(x):
        high = x.astype(BF16)
        return high, (x - high.astype(F32)).astype(BF16)

    def mix_copy(to):
        return remote(mix_send.at[to], mix_own.at[me], m_send.at[to], m_got.at[me], (base + to, tp))

    def combine(i, carry):
        s = (me + i + 1) % GROUP
        picks = pick_out[s]
        base_out = near_out[s]
        first, rest = split(picks[:, 1:2])
        first = first.astype(F32)
        second, third = split(picks[:, 1:2] - first)
        terms = jnp.concatenate(
            [
                jnp.where(mine, first, 0.0).astype(BF16),
                jnp.where(mine, second.astype(F32), 0.0).astype(BF16),
                jnp.where(mine, third.astype(F32), 0.0).astype(BF16),
            ],
            axis=1,
        )
        spread = mm(choose_t[...], terms)
        tops = spread[:, 0:128] + spread[:, 128:256] + spread[:, 256:384]
        tops = jnp.where(lane == 0, base_out[:, 1:2], jnp.where(covered == 1, tops, MASKED))
        top = jnp.max(tops, axis=1, keepdims=True)
        share = jnp.exp2((tops - top) * EXPONENT)
        high, rest = split(share)
        back = mm(choose[...], jnp.concatenate([high, rest], axis=1))
        back = back[:, 0:128] + back[:, 128:256]
        mass = jnp.sum(jnp.where(mine, back, 0.0), axis=1, keepdims=True)
        high, rest = split(jnp.where(lane == 1, 0.0, picks) * mass)
        more = mm(choose_t[...], jnp.concatenate([high, rest], axis=1))
        both = base_out * share[:, 0:1] + more[:, 0:128] + more[:, 128:256]
        mix = both / both[:, 0:1]
        packed = jnp.where(low_half, swap(mix[0:128]), mix[128:256]).astype(BF16)

        @pl.when(i < GROUP - 1)
        def _():
            mix_send[s] = packed
            mix_copy(s).start()

        @pl.when(i == GROUP - 1)
        def _():
            mix_own[me] = packed

        return carry

    lax.fori_loop(0, GROUP, combine, 0)

    def far_copy(h):
        return remote(mix_own.at[h], mix_far.at[h], f_send.at[h], f_got.at[h], partner)

    far_copy(me).start()

    def pass_on(i, carry):
        h = (me + GROUP - 1 - i) % GROUP
        remote(mix_send.at[h], mix_own.at[h], m_send.at[h], m_got.at[h], (base + h, tp)).wait_recv()
        far_copy(h).start()
        return carry

    lax.fori_loop(0, GROUP - 1, pass_on, 0)

    def widen(blocks):
        for pair in range(GROUP // 2):
            cut = slice(128 * pair, 128 * pair + 128)
            a = blocks[2 * pair].astype(F32)
            b = blocks[2 * pair + 1].astype(F32)
            mix_wide[0:128, cut] = jnp.where(low_half, a, swap(b)).astype(BF16)
            mix_wide[128:256, cut] = jnp.where(low_half, swap(a), b).astype(BF16)

    res_copy.wait_recv()
    widen(mix_own)
    for n in range(4):
        cut = slice(256 * n, 256 * n + 256)
        hidden[:, cut] = mm(mix_wide[...], out_weight[:, cut]) + res_all[
            n // 2, :, 256 * (n % 2) : 256 * (n % 2) + 256
        ].astype(F32)
    for copy in w_on:
        copy.wait_recv()

    def far_wait(h, carry):
        far_copy(h).wait_recv()
        return carry

    lax.fori_loop(0, GROUP, far_wait, 0)
    widen(mix_far)
    squares = jnp.zeros((ROWS, 1), F32)
    for n in range(4):
        cut = slice(256 * n, 256 * n + 256)
        h = hidden[:, cut] + mm(mix_wide[...], out_far[:, cut])
        hidden[:, cut] = h
        squares = squares + jnp.sum(h * h, axis=1, keepdims=True)
    inverse = lax.rsqrt(squares / 1024.0 + 1e-5)
    for n in range(4):
        cut = slice(256 * n, 256 * n + 256)
        normed[:, cut] = (hidden[:, cut] * inverse * gain[:, cut]).astype(BF16)

    loads[0].wait()
    loads[1].wait()

    def units(n, carry):
        cut = pl.ds(pl.multiple_of(n * 256, 256), 256)
        gate = mm(normed[...], gate_w[:, cut])
        up = mm(normed[...], up_w[:, cut])
        act[:, cut] = (gate / (1.0 + jnp.exp(-gate)) * up).astype(BF16)
        return carry

    lax.fori_loop(0, 4, units, 0)
    loads[2].wait()

    d_out = []
    for n in range(2):
        cut = pl.ds(pl.multiple_of((1 - tp) * COLS + n * 256, 256), 256)
        down_send[n] = mm(act[...], down_w[:, cut]).astype(BF16)
        d_out.append(remote(down_send.at[n], down_got.at[n], d_send.at[n], d_got.at[n], partner))
        d_out[-1].start()
    for n in range(2):
        cut = pl.ds(pl.multiple_of(tp * COLS + n * 256, 256), 256)
        hidden[:, cut] = hidden[:, cut] + mm(act[...], down_w[:, cut])
    for n in range(2):
        cut = pl.ds(pl.multiple_of(tp * COLS + n * 256, 256), 256)
        d_out[n].wait_recv()
        out[:, 256 * n : 256 * n + 256] = (hidden[:, cut] + down_got[n].astype(F32)).astype(BF16)

    for copy in a_out + w_out + w_on + [res_copy] + d_out:
        copy.wait_send()
    z_finish_send()

    def mix_sent(i, carry):
        mix_copy((me + i + 1) % GROUP).wait_send()
        return carry

    lax.fori_loop(0, GROUP - 1, mix_sent, 0)

    def far_sent(h, carry):
        far_copy(h).wait_send()
        return carry

    lax.fori_loop(0, GROUP, far_sent, 0)


def shards(
    residual_in,
    queries,
    keys,
    values,
    head_offset,
    out_weight,
    norm_gain,
    gate_weight,
    up_weight,
    down_weight,
):
    vmem = pl.BlockSpec(memory_space=pltpu.VMEM)
    smem = pl.BlockSpec(memory_space=pltpu.SMEM)
    hbm = pl.BlockSpec(memory_space=pl.ANY)
    dma = pltpu.SemaphoreType.DMA
    scratch = [
        pltpu.VMEM((GROUP, 384, 128), BF16),
        pltpu.VMEM((GROUP, 384, 128), BF16),
        pltpu.VMEM((6, ROWS, 128), BF16),
        pltpu.VMEM((6, ROWS, 128), BF16),
        pltpu.VMEM((6, ROWS, 128), BF16),
        pltpu.VMEM((448, 128), BF16),
        pltpu.VMEM((512, 128), BF16),
        pltpu.VMEM((512, 128), BF16),
        pltpu.VMEM((512, 128), BF16),
        pltpu.VMEM((GROUP, ROWS, 128), F32),
        pltpu.VMEM((GROUP, ROWS, 128), F32),
        pltpu.VMEM((ROWS, ROWS), BF16),
        pltpu.VMEM((ROWS, ROWS), BF16),
        pltpu.VMEM((GROUP, 128, 128), BF16),
        pltpu.VMEM((GROUP, 128, 128), BF16),
        pltpu.VMEM((GROUP, 128, 128), BF16),
        pltpu.VMEM((ROWS, COLS), BF16),
        pltpu.VMEM((2, ROWS, COLS), BF16),
        pltpu.VMEM((512, 1024), BF16),
        pltpu.VMEM((1024, 1024), BF16),
        pltpu.VMEM((1024, 1024), BF16),
        pltpu.VMEM((1024, 1024), BF16),
        pltpu.VMEM((ROWS, 1024), F32),
        pltpu.VMEM((ROWS, 1024), BF16),
        pltpu.VMEM((ROWS, 1024), BF16),
        pltpu.VMEM((2, ROWS, 256), BF16),
        pltpu.VMEM((2, ROWS, 256), BF16),
        dma((GROUP,)),
        dma((GROUP,)),
        dma((11,)),
        dma((11,)),
        dma((GROUP,)),
        dma((GROUP,)),
        dma((GROUP,)),
        dma((GROUP,)),
        dma((4,)),
        dma((4,)),
        dma,
        dma,
        dma((2,)),
        dma((2,)),
        dma((3,)),
    ]
    return pl.pallas_call(
        layer,
        out_shape=jax.ShapeDtypeStruct((ROWS, COLS), BF16),
        in_specs=[vmem, vmem, vmem, vmem, vmem, vmem, smem, hbm, hbm, hbm],
        out_specs=vmem,
        scratch_shapes=scratch,
        compiler_params=pltpu.CompilerParams(
            collective_id=0, has_side_effects=True, vmem_limit_bytes=48 * 2**20
        ),
        name="layer",
    )(
        queries,
        keys,
        values,
        residual_in,
        out_weight,
        norm_gain.reshape(1, 1024),
        head_offset,
        gate_weight,
        up_weight,
        down_weight,
    )


def solution(mesh):
    placed = (
        P("seq", "tp"),
        P("seq", "tp"),
        P("seq", "tp"),
        P("seq", "tp"),
        P(None, "tp"),
        P("tp", None),
        P(),
        P(None, "tp"),
        P(None, "tp"),
        P("tp", None),
    )
    return jax.shard_map(
        shards, mesh=mesh, in_specs=placed, out_specs=P("seq", "tp"), check_vma=False
    )
```

time: 372 us -> 62.9 us (0.17)
  the two profiles are of different devices: /device:TPU:1 before, /device:TPU:34 now
where the time goes in v1:
time: 62.9 us; the launch traced here: 62.5 us
  Pallas kernels  53.8 us (86%)
  local copies, waits for them, and re-layouts  8.69 us (14%)
    pallas_call x1, Pallas kernels, shards(): pl.pallas_call(layer, out_shape=jax.ShapeDtypeStruct((ROWS, COLS), BF16),...  53.8 us
    unnamed x17, local copies, waits for them, and re-layouts  8.69 us

profile of v1, /device:TPU:34, one launch (start us, length us, event | category | flops | bytes accessed | tf_op | source)
XLA Modules:
  0.0 62.5 jit_solution(7991051296080798435)
XLA Ops:
  0.0 0.0 copy-start
  0.0 1.6 %copy-done = bf16[1024,1024]{1,0:T(8,128)(2,1)S(1)} copy-done((bf16[1024,1024]{1,0:T(8,128)(2,1)S(1)}, bf16[1024,1024]{1,0:T(8,128)(2,1)}, u32[]{:S(2)}) %copy-start) | copy-done | bytes 2097176
  1.6 0.0 copy-start.1
  1.6 1.2 %copy-done.1 = bf16[512,1024]{1,0:T(8,128)(2,1)S(1)} copy-done((bf16[512,1024]{1,0:T(8,128)(2,1)S(1)}, bf16[512,1024]{1,0:T(8,128)(2,1)}, u32[]{:S(2)}) %copy-start.1) | copy-done | bytes 1048600
  2.8 0.0 copy-start.2
  2.8 0.9 %copy-done.2 = bf16[256,512]{1,0:T(8,128)(2,1)S(1)} copy-done((bf16[256,512]{1,0:T(8,128)(2,1)S(1)}, bf16[256,512]{1,0:T(8,128)(2,1)}, u32[]{:S(2)}) %copy-start.2) | copy-done | bytes 262168
  3.8 0.0 copy-start.3
  3.8 0.9 %copy-done.3 = bf16[256,512]{1,0:T(8,128)(2,1)S(1)} copy-done((bf16[256,512]{1,0:T(8,128)(2,1)S(1)}, bf16[256,512]{1,0:T(8,128)(2,1)}, u32[]{:S(2)}) %copy-start.3) | copy-done | bytes 262168
  4.7 0.0 copy-start.4
  4.7 0.9 %copy-done.4 = bf16[256,512]{1,0:T(8,128)(2,1)S(1)} copy-done((bf16[256,512]{1,0:T(8,128)(2,1)S(1)}, bf16[256,512]{1,0:T(8,128)(2,1)}, u32[]{:S(2)}) %copy-start.4) | copy-done | bytes 262168
  5.7 0.0 copy-start.5
  5.7 0.9 %copy-done.5 = bf16[256,512]{1,0:T(8,128)(2,1)S(1)} copy-done((bf16[256,512]{1,0:T(8,128)(2,1)S(1)}, bf16[256,512]{1,0:T(8,128)(2,1)}, u32[]{:S(2)}) %copy-start.5) | copy-done | bytes 262168
  6.6 0.0 copy-start.6
  6.6 0.7 %copy-done.6 = f32[1024]{0:T(1024)S(1)} copy-done((f32[1024]{0:T(1024)S(1)}, f32[1024]{0:T(1024)}, u32[]{:S(2)}) %copy-start.6) | copy-done | bytes 4120
  7.3 0.0 copy-start.7
  7.3 0.7 %copy-done.7 = s32[6,8]{1,0:T(8,128)S(1)} copy-done((s32[6,8]{1,0:T(8,128)S(1)}, s32[6,8]{1,0:T(8,128)}, u32[]{:S(2)}) %copy-start.7) | copy-done | bytes 216
  8.0 53.8 %layer.1 = bf16[256,512]{1,0:T(8,128)(2,1)S(1)} custom-call(bf16[256,512]{1,0:T(8,128)(2,1)S(1)} %copy-done.2, bf16[256,512]{1,0:T(8,128)(2,1)S(1)} %copy-done.3, bf16[256,512]{1,0:T(8,128)(2,1)S(1)} %copy-done.4, bf16[256,512]{1,0:T(8,128)(2,1)S(1)} %copy-done.5, bf16[512,1024]{1,0:T(8,128)(2,1)S(1)} %copy-done.1, f32[1,1024]{1,0:T(1,128)S(1)} %bitcast.1, ...), custom_call_target="tpu_custom_call" | custom-call | tf_op jit(solution)/shard_map/layer/pallas_call | solution.py:584
  61.8 0.7 %copy.12 = bf16[256,512]{1,0:T(8,128)(2,1)} copy(bf16[256,512]{1,0:T(8,128)(2,1)S(1)} %layer.1) | data formatting | bytes 524288
Async XLA Ops:
  0.0 1.6 %copy-start = (bf16[1024,1024]{1,0:T(8,128)(2,1)S(1)}, bf16[1024,1024]{1,0:T(8,128)(2,1)}, u32[]{:S(2)}) copy-start(bf16[1024,1024]{1,0:T(8,128)(2,1)} %gate_hbm.1) | copy-start | bytes 6291460
  1.6 1.2 %copy-start.1 = (bf16[512,1024]{1,0:T(8,128)(2,1)S(1)}, bf16[512,1024]{1,0:T(8,128)(2,1)}, u32[]{:S(2)}) copy-start(bf16[512,1024]{1,0:T(8,128)(2,1)} %out_weight.1) | copy-start | bytes 3145732
  2.8 0.9 %copy-start.2 = (bf16[256,512]{1,0:T(8,128)(2,1)S(1)}, bf16[256,512]{1,0:T(8,128)(2,1)}, u32[]{:S(2)}) copy-start(bf16[256,512]{1,0:T(8,128)(2,1)} %queries.1) | copy-start | bytes 786436
  3.8 0.9 %copy-start.3 = (bf16[256,512]{1,0:T(8,128)(2,1)S(1)}, bf16[256,512]{1,0:T(8,128)(2,1)}, u32[]{:S(2)}) copy-start(bf16[256,512]{1,0:T(8,128)(2,1)} %keys.1) | copy-start | bytes 786436
  4.7 0.9 %copy-start.4 = (bf16[256,512]{1,0:T(8,128)(2,1)S(1)}, bf16[256,512]{1,0:T(8,128)(2,1)}, u32[]{:S(2)}) copy-start(bf16[256,512]{1,0:T(8,128)(2,1)} %values.1) | copy-start | bytes 786436
  5.7 0.9 %copy-start.5 = (bf16[256,512]{1,0:T(8,128)(2,1)S(1)}, bf16[256,512]{1,0:T(8,128)(2,1)}, u32[]{:S(2)}) copy-start(bf16[256,512]{1,0:T(8,128)(2,1)} %residual.1) | copy-start | bytes 786436
  6.6 0.7 %copy-start.6 = (f32[1024]{0:T(1024)S(1)}, f32[1024]{0:T(1024)}, u32[]{:S(2)}) copy-start(f32[1024]{0:T(1024)} %param.16) | copy-start | bytes 12292
  7.3 0.7 %copy-start.7 = (s32[6,8]{1,0:T(8,128)S(1)}, s32[6,8]{1,0:T(8,128)}, u32[]{:S(2)}) copy-start(s32[6,8]{1,0:T(8,128)} %offsets.1) | copy-start | bytes 580

commit v2 on v1

--- a/solution.py
+++ b/solution.py
@@ -15,6 +15,7 @@
 COLS = 512
 GROUP = 8
 ZED = 8
+LAG = 2
 MASKED = -1e30
 EXPONENT = math.log2(math.e) / 8.0
 
@@ -50,17 +51,22 @@
 
 
 def layer(
-    queries,
-    keys,
-    values,
-    residual,
-    out_weight,
-    gain,
+    q_hbm,
+    k_hbm,
+    v_hbm,
+    res_hbm,
+    out_hbm,
+    gain_hbm,
     offsets,
     gate_hbm,
     up_hbm,
     down_hbm,
     out,
+    queries,
+    keys,
+    values,
+    gain,
+    out_weight,
     send,
     got,
     pick_kv,
@@ -88,6 +94,7 @@
     act,
     down_send,
     down_got,
+    shares,
     a_send,
     a_got,
     z_send,
@@ -123,10 +130,23 @@
         )
 
     loads = [
-        pltpu.make_async_copy(gate_hbm, gate_w, local.at[0]),
-        pltpu.make_async_copy(up_hbm, up_w, local.at[1]),
-        pltpu.make_async_copy(down_hbm, down_w, local.at[2]),
+        pltpu.make_async_copy(src, dst, local.at[i])
+        for i, (src, dst) in enumerate(
+            (
+                (gate_hbm, gate_w),
+                (up_hbm, up_w),
+                (down_hbm, down_w),
+                (k_hbm, keys),
+                (v_hbm, values),
+                (q_hbm, queries),
+                (out_hbm, out_weight),
+                (res_hbm, res_all.at[tp]),
+                (gain_hbm, gain),
+            )
+        )
     ]
+    for load in loads[3:6]:
+        load.start()
 
     k3[...] = jnp.zeros_like(k3)
     k4[...] = jnp.zeros_like(k4)
@@ -143,8 +163,9 @@
 
     low = lanes((ROWS, 128)) < 64
     low_half = lanes((128, 128)) < 64
-    for pair in range(GROUP // 2):
-        cut = slice(128 * pair, 128 * pair + 128)
+
+    def pack(pair):
+        cut = pl.ds(pl.multiple_of(128 * pair, 128), 128)
         k = keys[:, cut].astype(F32)
         v = values[:, cut].astype(F32)
         q = queries[:, cut].astype(F32)
@@ -154,18 +175,26 @@
         send[2 * pair, ROWS : ROWS + 128] = jnp.where(low_half, top, swap(bottom)).astype(BF16)
         send[2 * pair + 1, ROWS : ROWS + 128] = jnp.where(low_half, swap(top), bottom).astype(BF16)
 
-    pl.semaphore_wait(barrier, 2 * (GROUP - 1) + 2)
-
     def block_copy(to):
         return remote(send.at[to], got.at[me], a_send.at[to], a_got.at[me], (base + to, tp))
 
-    a_out = []
-    for step in (2, 1, 3):
+    for load in loads[3:6]:
+        load.wait()
+    pack((y + 2) % 4)
+    pl.semaphore_wait(barrier, 2 * (GROUP - 1) + 2)
+
+    def post(step):
         for c in range(2):
-            a_out.append(block_copy(((y + step) % 4) * 2 + c))
-            a_out[-1].start()
-    a_out.append(block_copy(me + 1 - 2 * core))
-    a_out[-1].start()
+            block_copy(((y + step) % 4) * 2 + c).start()
+
+    post(2)
+    pack((y + 1) % 4)
+    post(1)
+    pack((y + 3) % 4)
+    post(3)
+    pack(y)
+    a_last = block_copy(me + 1 - 2 * core)
+    a_last.start()
     got[me] = send[me]
 
     w_first = core * 128
@@ -175,14 +204,13 @@
         piece = pl.ds(pl.multiple_of(first, 128), 128)
         return remote(src.at[piece], out_far.at[piece], w_send.at[i], w_got.at[i], to)
 
-    w_out = [w_piece(w_first, 0, partner, out_weight), w_piece(w_second, 1, behind, out_weight)]
-    res_copy = remote(residual, res_all.at[tp], r_send, r_got, partner)
+    w_out = [w_piece(w_first, 0, partner, out_hbm), w_piece(w_second, 1, behind, out_hbm)]
+    res_copy = remote(res_hbm, res_all.at[tp], r_send, r_got, partner)
     res_copy.start()
     for copy in w_out:
         copy.start()
-    for load in loads:
+    for load in loads[0:3] + loads[6:]:
         load.start()
-    res_all[tp] = residual[...]
 
     def target(i):
         spot = jnp.full(i.shape, -1, jnp.int32)
@@ -266,7 +294,7 @@
         return finish(mm(p00, v0), t0), finish(mm(p10, v0) + mm(p11, v1), t1)
 
     def near(m, carry):
-        j = (y + m + (m // 2) * (5 - 2 * m)) % 4
+        j = (y + (m % 3 + 1) * ((m + 3) // 4)) % 4
 
         def wait(s):
             remote(send.at[s], got.at[s], a_send.at[s], a_got.at[s], (base + s, tp)).wait_recv()
@@ -372,139 +400,184 @@
 
     tile = (ROWS, 128)
     lane = lanes(tile)
-    mine = lane == branch_of(sublanes(tile))
+    branch = branch_of(sublanes(tile))
+    mine = lane % 16 == branch
     covered = jnp.zeros(tile, jnp.int32)
     for b in range(1, 6):
         off = offsets[b, me] & (2**b - 1)
         hit = jnp.where(sublanes(tile) % 2**b == off, 1, 0)
-        covered = jnp.where(lane == b, hit, covered)
+        covered = jnp.where(lane % 16 == b, hit, covered)
 
     def split(x):
         high = x.astype(BF16)
         return high, (x - high.astype(F32)).astype(BF16)
 
+    tops = jnp.zeros(tile, F32)
+    bases = jnp.zeros(tile, F32)
+    for s in range(GROUP):
+        here = lane // 16 == s
+        tops = jnp.where(here, pick_out[s, :, 1:2], tops)
+        bases = jnp.where(here, near_out[s, :, 1:2], bases)
+    first, rest = split(jnp.where(mine, tops, 0.0))
+    second, third = split(jnp.where(mine, tops, 0.0) - first.astype(F32))
+    spread = mm(choose_t[...], jnp.concatenate([first, second, third], axis=1))
+    tops = spread[:, 0:128] + spread[:, 128:256] + spread[:, 256:384]
+    tops = jnp.where(lane % 16 == 0, bases, jnp.where(covered == 1, tops, MASKED))
+    top = tops
+    for shift in (1, 2, 4):
+        top = jnp.maximum(top, pltpu.roll(top, shift, 1))
+    for shift in (127, 126, 124):
+        top = jnp.maximum(top, pltpu.roll(top, shift, 1))
+    share = jnp.exp2((tops - top) * EXPONENT)
+    high, rest = split(share)
+    back = mm(choose[...], jnp.concatenate([high, rest], axis=1))
+    shares[0] = share
+    shares[1] = jnp.where(mine, back[:, 0:128] + back[:, 128:256], 0.0)
+
     def mix_copy(to):
         return remote(mix_send.at[to], mix_own.at[me], m_send.at[to], m_got.at[me], (base + to, tp))
 
+    def mix_wait(h):
+        remote(mix_send.at[h], mix_own.at[h], m_send.at[h], m_got.at[h], (base + h, tp)).wait_recv()
+
+    def far_copy(h, r):
+        return remote(
+            mix_own.at[h, r], mix_far.at[h, r], f_send.at[2 * h + r], f_got.at[2 * h + r], partner
+        )
+
+    small = lanes((64, 128)) < 64
+
     def combine(i, carry):
         s = (me + i + 1) % GROUP
-        picks = pick_out[s]
-        base_out = near_out[s]
-        first, rest = split(picks[:, 1:2])
-        first = first.astype(F32)
-        second, third = split(picks[:, 1:2] - first)
-        terms = jnp.concatenate(
-            [
-                jnp.where(mine, first, 0.0).astype(BF16),
-                jnp.where(mine, second.astype(F32), 0.0).astype(BF16),
-                jnp.where(mine, third.astype(F32), 0.0).astype(BF16),
-            ],
-            axis=1,
-        )
-        spread = mm(choose_t[...], terms)
-        tops = spread[:, 0:128] + spread[:, 128:256] + spread[:, 256:384]
-        tops = jnp.where(lane == 0, base_out[:, 1:2], jnp.where(covered == 1, tops, MASKED))
-        top = jnp.max(tops, axis=1, keepdims=True)
-        share = jnp.exp2((tops - top) * EXPONENT)
-        high, rest = split(share)
-        back = mm(choose[...], jnp.concatenate([high, rest], axis=1))
-        back = back[:, 0:128] + back[:, 128:256]
-        mass = jnp.sum(jnp.where(mine, back, 0.0), axis=1, keepdims=True)
-        high, rest = split(jnp.where(lane == 1, 0.0, picks) * mass)
-        more = mm(choose_t[...], jnp.concatenate([high, rest], axis=1))
-        both = base_out * share[:, 0:1] + more[:, 0:128] + more[:, 128:256]
+        here = lane // 16 == s
+        near_share = jnp.sum(jnp.where(lane == 16 * s, shares[0], 0.0), axis=1, keepdims=True)
+        mass = jnp.sum(jnp.where(here, shares[1], 0.0), axis=1, keepdims=True)
+        both = near_out[s] * near_share + mm(choose_t[...], (pick_out[s] * mass).astype(BF16))
         mix = both / both[:, 0:1]
-        packed = jnp.where(low_half, swap(mix[0:128]), mix[128:256]).astype(BF16)
+        halves = [
+            jnp.where(small, swap(mix[128 * r : 128 * r + 64]), mix[128 * r + 64 : 128 * r + 128]).astype(
+                BF16
+            )
+            for r in range(2)
+        ]
 
         @pl.when(i < GROUP - 1)
         def _():
-            mix_send[s] = packed
+            for r in range(2):
+                mix_send[s, r] = halves[r]
             mix_copy(s).start()
 
         @pl.when(i == GROUP - 1)
         def _():
-            mix_own[me] = packed
+            for r in range(2):
+                mix_own[me, r] = halves[r]
+            far_copy(me, 0).start()
+
+        @pl.when(i >= LAG)
+        def _():
+            h = (me + GROUP - 1 - (i - LAG)) % GROUP
+            mix_wait(h)
+            far_copy(h, 0).start()
 
         return carry
 
     lax.fori_loop(0, GROUP, combine, 0)
-
-    def far_copy(h):
-        return remote(mix_own.at[h], mix_far.at[h], f_send.at[h], f_got.at[h], partner)
-
-    far_copy(me).start()
 
     def pass_on(i, carry):
         h = (me + GROUP - 1 - i) % GROUP
-        remote(mix_send.at[h], mix_own.at[h], m_send.at[h], m_got.at[h], (base + h, tp)).wait_recv()
-        far_copy(h).start()
-        return carry
-
-    lax.fori_loop(0, GROUP - 1, pass_on, 0)
-
-    def widen(blocks):
+        mix_wait(h)
+        far_copy(h, 0).start()
+        return carry
+
+    lax.fori_loop(GROUP - LAG, GROUP - 1, pass_on, 0)
+
+    def pass_second(h, carry):
+        far_copy(h, 1).start()
+        return carry
+
+    lax.fori_loop(0, GROUP, pass_second, 0)
+
+    def widen(blocks, r):
         for pair in range(GROUP // 2):
             cut = slice(128 * pair, 128 * pair + 128)
-            a = blocks[2 * pair].astype(F32)
-            b = blocks[2 * pair + 1].astype(F32)
-            mix_wide[0:128, cut] = jnp.where(low_half, a, swap(b)).astype(BF16)
-            mix_wide[128:256, cut] = jnp.where(low_half, swap(a), b).astype(BF16)
+            a = blocks[2 * pair, r].astype(F32)
+            b = blocks[2 * pair + 1, r].astype(F32)
+            mix_wide[r, 0:64, cut] = jnp.where(small, a, swap(b)).astype(BF16)
+            mix_wide[r, 64:128, cut] = jnp.where(small, swap(a), b).astype(BF16)
 
     res_copy.wait_recv()
-    widen(mix_own)
-    for n in range(4):
-        cut = slice(256 * n, 256 * n + 256)
-        hidden[:, cut] = mm(mix_wide[...], out_weight[:, cut]) + res_all[
-            n // 2, :, 256 * (n % 2) : 256 * (n % 2) + 256
-        ].astype(F32)
+    for load in loads[6:]:
+        load.wait()
+
+    def near_hidden(r, carry):
+        widen(mix_own, r)
+        for n in range(4):
+            cut = slice(256 * n, 256 * n + 256)
+            rows = pl.ds(pl.multiple_of(128 * r, 128), 128)
+            half_cut = slice(256 * (n % 2), 256 * (n % 2) + 256)
+            hidden[r, :, cut] = mm(mix_wide[r], out_weight[:, cut]) + res_all[
+                n // 2, rows, half_cut
+            ].astype(F32)
+        return carry
+
+    lax.fori_loop(0, 2, near_hidden, 0)
     for copy in w_on:
         copy.wait_recv()
-
-    def far_wait(h, carry):
-        far_copy(h).wait_recv()
-        return carry
-
-    lax.fori_loop(0, GROUP, far_wait, 0)
-    widen(mix_far)
-    squares = jnp.zeros((ROWS, 1), F32)
-    for n in range(4):
-        cut = slice(256 * n, 256 * n + 256)
-        h = hidden[:, cut] + mm(mix_wide[...], out_far[:, cut])
-        hidden[:, cut] = h
-        squares = squares + jnp.sum(h * h, axis=1, keepdims=True)
-    inverse = lax.rsqrt(squares / 1024.0 + 1e-5)
-    for n in range(4):
-        cut = slice(256 * n, 256 * n + 256)
-        normed[:, cut] = (hidden[:, cut] * inverse * gain[:, cut]).astype(BF16)
-
-    loads[0].wait()
-    loads[1].wait()
-
-    def units(n, carry):
-        cut = pl.ds(pl.multiple_of(n * 256, 256), 256)
-        gate = mm(normed[...], gate_w[:, cut])
-        up = mm(normed[...], up_w[:, cut])
-        act[:, cut] = (gate / (1.0 + jnp.exp(-gate)) * up).astype(BF16)
-        return carry
-
-    lax.fori_loop(0, 4, units, 0)
-    loads[2].wait()
-
-    d_out = []
-    for n in range(2):
-        cut = pl.ds(pl.multiple_of((1 - tp) * COLS + n * 256, 256), 256)
-        down_send[n] = mm(act[...], down_w[:, cut]).astype(BF16)
-        d_out.append(remote(down_send.at[n], down_got.at[n], d_send.at[n], d_got.at[n], partner))
-        d_out[-1].start()
-    for n in range(2):
-        cut = pl.ds(pl.multiple_of(tp * COLS + n * 256, 256), 256)
-        hidden[:, cut] = hidden[:, cut] + mm(act[...], down_w[:, cut])
-    for n in range(2):
-        cut = pl.ds(pl.multiple_of(tp * COLS + n * 256, 256), 256)
-        d_out[n].wait_recv()
-        out[:, 256 * n : 256 * n + 256] = (hidden[:, cut] + down_got[n].astype(F32)).astype(BF16)
-
-    for copy in a_out + w_out + w_on + [res_copy] + d_out:
+    for load in loads[0:3]:
+        load.wait()
+
+    def down_copy(r, n):
+        return remote(
+            down_send.at[r, n], down_got.at[r, n], d_send.at[2 * r + n], d_got.at[2 * r + n], partner
+        )
+
+    def feed(r, carry):
+        def far_wait(h, carry):
+            far_copy(h, r).wait_recv()
+            return carry
+
+        lax.fori_loop(0, GROUP, far_wait, 0)
+        widen(mix_far, r)
+        squares = jnp.zeros((128, 1), F32)
+        for n in range(4):
+            cut = slice(256 * n, 256 * n + 256)
+            h = hidden[r, :, cut] + mm(mix_wide[r], out_far[:, cut])
+            hidden[r, :, cut] = h
+            squares = squares + jnp.sum(h * h, axis=1, keepdims=True)
+        inverse = lax.rsqrt(squares / 1024.0 + 1e-5)
+        for n in range(4):
+            cut = slice(256 * n, 256 * n + 256)
+            normed[r, :, cut] = (hidden[r, :, cut] * inverse * gain[:, cut]).astype(BF16)
+        for n in range(4):
+            cut = slice(256 * n, 256 * n + 256)
+            gate = mm(normed[r], gate_w[:, cut])
+            up = mm(normed[r], up_w[:, cut])
+            act[r, :, cut] = (gate / (1.0 + jnp.exp(-gate)) * up).astype(BF16)
+        for n in range(2):
+            cut = pl.ds(pl.multiple_of((1 - tp) * COLS + n * 256, 256), 256)
+            down_send[r, n] = mm(act[r], down_w[:, cut]).astype(BF16)
+            down_copy(r, n).start()
+        return carry
+
+    lax.fori_loop(0, 2, feed, 0)
+
+    def last(r, carry):
+        rows = pl.ds(pl.multiple_of(128 * r, 128), 128)
+        for n in range(2):
+            cut = pl.ds(pl.multiple_of(tp * COLS + n * 256, 256), 256)
+            own = hidden[r, :, cut] + mm(act[r], down_w[:, cut])
+            down_copy(r, n).wait_recv()
+            out[rows, 256 * n : 256 * n + 256] = (own + down_got[r, n].astype(F32)).astype(BF16)
+        return carry
+
+    lax.fori_loop(0, 2, last, 0)
+
+    def block_sent(k, carry):
+        block_copy((me + k) % GROUP).wait_send()
+        return carry
+
+    lax.fori_loop(1, GROUP, block_sent, 0)
+    for copy in w_out + w_on + [res_copy]:
         copy.wait_send()
     z_finish_send()
 
@@ -515,10 +588,14 @@
     lax.fori_loop(0, GROUP - 1, mix_sent, 0)
 
     def far_sent(h, carry):
-        far_copy(h).wait_send()
+        for r in range(2):
+            far_copy(h, r).wait_send()
         return carry
 
     lax.fori_loop(0, GROUP, far_sent, 0)
+    for r in range(2):
+        for n in range(2):
+            down_copy(r, n).wait_send()
 
 
 def shards(
@@ -538,6 +615,11 @@
     hbm = pl.BlockSpec(memory_space=pl.ANY)
     dma = pltpu.SemaphoreType.DMA
     scratch = [
+        pltpu.VMEM((ROWS, COLS), BF16),
+        pltpu.VMEM((ROWS, COLS), BF16),
+        pltpu.VMEM((ROWS, COLS), BF16),
+        pltpu.VMEM((1, 1024), F32),
+        pltpu.VMEM((512, 1024), BF16),
         pltpu.VMEM((GROUP, 384, 128), BF16),
         pltpu.VMEM((GROUP, 384, 128), BF16),
         pltpu.VMEM((6, ROWS, 128), BF16),
@@ -551,44 +633,45 @@
         pltpu.VMEM((GROUP, ROWS, 128), F32),
         pltpu.VMEM((ROWS, ROWS), BF16),
         pltpu.VMEM((ROWS, ROWS), BF16),
-        pltpu.VMEM((GROUP, 128, 128), BF16),
-        pltpu.VMEM((GROUP, 128, 128), BF16),
-        pltpu.VMEM((GROUP, 128, 128), BF16),
-        pltpu.VMEM((ROWS, COLS), BF16),
+        pltpu.VMEM((GROUP, 2, 64, 128), BF16),
+        pltpu.VMEM((GROUP, 2, 64, 128), BF16),
+        pltpu.VMEM((GROUP, 2, 64, 128), BF16),
+        pltpu.VMEM((2, 128, COLS), BF16),
         pltpu.VMEM((2, ROWS, COLS), BF16),
         pltpu.VMEM((512, 1024), BF16),
         pltpu.VMEM((1024, 1024), BF16),
         pltpu.VMEM((1024, 1024), BF16),
         pltpu.VMEM((1024, 1024), BF16),
-        pltpu.VMEM((ROWS, 1024), F32),
-        pltpu.VMEM((ROWS, 1024), BF16),
-        pltpu.VMEM((ROWS, 1024), BF16),
-        pltpu.VMEM((2, ROWS, 256), BF16),
-        pltpu.VMEM((2, ROWS, 256), BF16),
+        pltpu.VMEM((2, 128, 1024), F32),
+        pltpu.VMEM((2, 128, 1024), BF16),
+        pltpu.VMEM((2, 128, 1024), BF16),
+        pltpu.VMEM((2, 2, 128, 256), BF16),
+        pltpu.VMEM((2, 2, 128, 256), BF16),
+        pltpu.VMEM((2, ROWS, 128), F32),
         dma((GROUP,)),
         dma((GROUP,)),
         dma((11,)),
         dma((11,)),
         dma((GROUP,)),
         dma((GROUP,)),
-        dma((GROUP,)),
-        dma((GROUP,)),
+        dma((2 * GROUP,)),
+        dma((2 * GROUP,)),
         dma((4,)),
         dma((4,)),
         dma,
         dma,
-        dma((2,)),
-        dma((2,)),
-        dma((3,)),
+        dma((4,)),
+        dma((4,)),
+        dma((9,)),
     ]
     return pl.pallas_call(
         layer,
         out_shape=jax.ShapeDtypeStruct((ROWS, COLS), BF16),
-        in_specs=[vmem, vmem, vmem, vmem, vmem, vmem, smem, hbm, hbm, hbm],
+        in_specs=[hbm, hbm, hbm, hbm, hbm, hbm, smem, hbm, hbm, hbm],
         out_specs=vmem,
         scratch_shapes=scratch,
         compiler_params=pltpu.CompilerParams(
-            collective_id=0, has_side_effects=True, vmem_limit_bytes=48 * 2**20
+            collective_id=0, has_side_effects=True, vmem_limit_bytes=60 * 2**20
         ),
         name="layer",
     )(

time: 62.9 us -> 51.7 us (0.82)
  local copies, waits for them, and re-layouts: 8.69 us -> 1.67 us
  Pallas kernels: 53.8 us -> 49.5 us
    unnamed x17 -> x1, local copies, waits for them, and re-layouts: 8.69 us -> 1.67 us
    pallas_call x1, Pallas kernels: 53.8 us -> 49.5 us  [shards(): pl.pallas_call(layer, out_shape=jax.ShapeDtypeStruct((ROWS, COLS), BF16),...]
where the time goes in v2:
time: 51.7 us; the launch traced here: 51.1 us
  Pallas kernels  49.5 us (96%)
  local copies, waits for them, and re-layouts  1.67 us (3%)
    pallas_call x1, Pallas kernels, shards(): pl.pallas_call(layer, out_shape=jax.ShapeDtypeStruct((ROWS, COLS), BF16),...  49.5 us
    unnamed x1, local copies, waits for them, and re-layouts  1.67 us

profile of v2, /device:TPU:34, one launch (start us, length us, event | category | flops | bytes accessed | tf_op | source)
XLA Modules:
  0.0 51.1 jit_solution(12840439184514530764)
XLA Ops:
  0.0 49.5 %layer.1 = bf16[256,512]{1,0:T(8,128)(2,1)} custom-call(bf16[256,512]{1,0:T(8,128)(2,1)} %q_hbm.1, bf16[256,512]{1,0:T(8,128)(2,1)} %k_hbm.1, bf16[256,512]{1,0:T(8,128)(2,1)} %v_hbm.1, bf16[256,512]{1,0:T(8,128)(2,1)} %res_hbm.1, bf16[512,1024]{1,0:T(8,128)(2,1)} %out_hbm.1, f32[1,1024]{1,0:T(1,128)} %bitcast.1, s32[6,8]{1,0:T(8,128)} %offsets.1, ...), custom_call_target="tpu_custom_call" | custom-call | tf_op jit(solution)/shard_map/layer/pallas_call | solution.py:667
  49.5 1.7 %copy.12 = bf16[256,512]{1,0:T(8,128)(2,1)} copy(bf16[256,512]{1,0:T(8,128)(2,1)} %layer.1) | data formatting | bytes 524288

commit v3 on v2

--- a/solution.py
+++ b/solution.py
@@ -15,7 +15,6 @@
 COLS = 512
 GROUP = 8
 ZED = 8
-LAG = 2
 MASKED = -1e30
 EXPONENT = math.log2(math.e) / 8.0
 
@@ -95,6 +94,7 @@
     down_send,
     down_got,
     shares,
+    weighed,
     a_send,
     a_got,
     z_send,
@@ -110,6 +110,8 @@
     d_send,
     d_got,
     local,
+    here_sem,
+    all_sem,
 ):
     seq = lax.axis_index("seq")
     tp = lax.axis_index("tp")
@@ -152,14 +154,44 @@
     k4[...] = jnp.zeros_like(k4)
     k5[...] = jnp.zeros_like(k5)
     barrier = pltpu.get_barrier_semaphore()
+    lead = me == 0
+
+    def greet(device):
+        pl.semaphore_signal(barrier, inc=1, device_id=device, device_id_type=MESH)
+
     for k in range(1, GROUP):
-        pl.semaphore_signal(barrier, inc=1, device_id=(base + (me + k) % GROUP, tp), device_id_type=MESH)
-    for d in range(1, ZED):
-        pl.semaphore_signal(
-            barrier, inc=1, device_id=(plane + ((z + d) % ZED) * GROUP + me, tp), device_id_type=MESH
-        )
-    pl.semaphore_signal(barrier, inc=1, device_id=partner, device_id_type=MESH)
-    pl.semaphore_signal(barrier, inc=1, device_id=behind, device_id_type=MESH)
+        to = (me + k) % GROUP
+
+        @pl.when(to != 0)
+        def _():
+            greet((base + to, tp))
+
+    greet(partner)
+    greet(behind)
+
+    def group_entered():
+        @pl.when(lead)
+        def _():
+            pl.semaphore_wait(here_sem, GROUP - 1)
+
+        @pl.when(me != 0)
+        def _():
+            pl.semaphore_wait(barrier, GROUP + 1)
+            pl.semaphore_signal(here_sem, inc=1, device_id=(base, tp), device_id_type=MESH)
+
+    def all_entered():
+        @pl.when(lead)
+        def _():
+            for d in range(1, ZED):
+                greet((plane + ((z + d) % ZED) * GROUP, tp))
+            pl.semaphore_wait(barrier, ZED + 1)
+            for k in range(1, GROUP):
+                pl.semaphore_signal(all_sem, inc=1, device_id=(base + k, tp), device_id_type=MESH)
+
+    def all_known():
+        @pl.when(me != 0)
+        def _():
+            pl.semaphore_wait(all_sem, 1)
 
     low = lanes((ROWS, 128)) < 64
     low_half = lanes((128, 128)) < 64
@@ -181,7 +213,7 @@
     for load in loads[3:6]:
         load.wait()
     pack((y + 2) % 4)
-    pl.semaphore_wait(barrier, 2 * (GROUP - 1) + 2)
+    group_entered()
 
     def post(step):
         for c in range(2):
@@ -196,6 +228,7 @@
     a_last = block_copy(me + 1 - 2 * core)
     a_last.start()
     got[me] = send[me]
+    all_entered()
 
     w_first = core * 128
     w_second = 256 + core * 128
@@ -339,6 +372,7 @@
 
         @pl.when(m == 3)
         def _():
+            all_known()
             z_start()
 
         o0, o1 = causal_pair(qs[0], qs[1], kvs[0], kvs[1], v1s[0], v1s[1])
@@ -434,68 +468,70 @@
     shares[0] = share
     shares[1] = jnp.where(mine, back[:, 0:128] + back[:, 128:256], 0.0)
 
-    def mix_copy(to):
-        return remote(mix_send.at[to], mix_own.at[me], m_send.at[to], m_got.at[me], (base + to, tp))
-
-    def mix_wait(h):
-        remote(mix_send.at[h], mix_own.at[h], m_send.at[h], m_got.at[h], (base + h, tp)).wait_recv()
-
-    def far_copy(h, r):
+    def mix_copy(to, r):
         return remote(
-            mix_own.at[h, r], mix_far.at[h, r], f_send.at[2 * h + r], f_got.at[2 * h + r], partner
+            mix_send.at[to, r],
+            mix_own.at[me, r],
+            m_send.at[2 * to + r],
+            m_got.at[2 * me + r],
+            (base + to, tp),
         )
 
+    def mix_wait(h, r):
+        remote(
+            mix_send.at[h, r], mix_own.at[h, r], m_send.at[2 * h + r], m_got.at[2 * h + r], (base + h, tp)
+        ).wait_recv()
+
+    def far_copy(to, r):
+        return remote(
+            mix_send.at[to, r],
+            mix_far.at[me, r],
+            f_send.at[2 * to + r],
+            f_got.at[2 * me + r],
+            (base + to, 1 - tp),
+        )
+
+    def far_wait(h, r):
+        remote(
+            mix_send.at[h, r],
+            mix_far.at[h, r],
+            f_send.at[2 * h + r],
+            f_got.at[2 * h + r],
+            (base + h, 1 - tp),
+        ).wait_recv()
+
     small = lanes((64, 128)) < 64
 
+    def weigh(s, carry):
+        mass = jnp.sum(jnp.where(lane // 16 == s, shares[1], 0.0), axis=1, keepdims=True)
+        weighed[s] = (pick_out[s] * mass).astype(BF16)
+        return carry
+
+    lax.fori_loop(0, GROUP, weigh, 0)
+
     def combine(i, carry):
-        s = (me + i + 1) % GROUP
-        here = lane // 16 == s
-        near_share = jnp.sum(jnp.where(lane == 16 * s, shares[0], 0.0), axis=1, keepdims=True)
-        mass = jnp.sum(jnp.where(here, shares[1], 0.0), axis=1, keepdims=True)
-        both = near_out[s] * near_share + mm(choose_t[...], (pick_out[s] * mass).astype(BF16))
+        r = i // GROUP
+        s = (me + i + 3) % GROUP
+        rows = pl.ds(pl.multiple_of(128 * r, 128), 128)
+        near_share = jnp.sum(
+            jnp.where(lanes((128, 128)) == 16 * s, shares[0, rows], 0.0), axis=1, keepdims=True
+        )
+        both = near_out[s, rows] * near_share + mm(choose_t[rows], weighed[s])
         mix = both / both[:, 0:1]
-        halves = [
-            jnp.where(small, swap(mix[128 * r : 128 * r + 64]), mix[128 * r + 64 : 128 * r + 128]).astype(
-                BF16
-            )
-            for r in range(2)
-        ]
-
-        @pl.when(i < GROUP - 1)
-        def _():
-            for r in range(2):
-                mix_send[s, r] = halves[r]
-            mix_copy(s).start()
-
-        @pl.when(i == GROUP - 1)
-        def _():
-            for r in range(2):
-                mix_own[me, r] = halves[r]
-            far_copy(me, 0).start()
-
-        @pl.when(i >= LAG)
-        def _():
-            h = (me + GROUP - 1 - (i - LAG)) % GROUP
-            mix_wait(h)
-            far_copy(h, 0).start()
-
-        return carry
-
-    lax.fori_loop(0, GROUP, combine, 0)
-
-    def pass_on(i, carry):
-        h = (me + GROUP - 1 - i) % GROUP
-        mix_wait(h)
-        far_copy(h, 0).start()
-        return carry
-
-    lax.fori_loop(GROUP - LAG, GROUP - 1, pass_on, 0)
-
-    def pass_second(h, carry):
-        far_copy(h, 1).start()
-        return carry
-
-    lax.fori_loop(0, GROUP, pass_second, 0)
+        mix_send[s, r] = jnp.where(small, swap(mix[0:64]), mix[64:128]).astype(BF16)
+        far_copy(s, r).start()
+
+        @pl.when(s != me)
+        def _():
+            mix_copy(s, r).start()
+
+        @pl.when(s == me)
+        def _():
+            mix_own[me, r] = mix_send[me, r]
+
+        return carry
+
+    lax.fori_loop(0, 2 * GROUP, combine, 0)
 
     def widen(blocks, r):
         for pair in range(GROUP // 2):
@@ -510,6 +546,11 @@
         load.wait()
 
     def near_hidden(r, carry):
+        def own_wait(k, carry):
+            mix_wait((me + k) % GROUP, r)
+            return carry
+
+        lax.fori_loop(1, GROUP, own_wait, 0)
         widen(mix_own, r)
         for n in range(4):
             cut = slice(256 * n, 256 * n + 256)
@@ -532,11 +573,11 @@
         )
 
     def feed(r, carry):
-        def far_wait(h, carry):
-            far_copy(h, r).wait_recv()
+        def other_wait(h, carry):
+            far_wait(h, r)
             return carry
 
-        lax.fori_loop(0, GROUP, far_wait, 0)
+        lax.fori_loop(0, GROUP, other_wait, 0)
         widen(mix_far, r)
         squares = jnp.zeros((128, 1), F32)
         for n in range(4):
@@ -582,10 +623,11 @@
     z_finish_send()
 
     def mix_sent(i, carry):
-        mix_copy((me + i + 1) % GROUP).wait_send()
-        return carry
-
-    lax.fori_loop(0, GROUP - 1, mix_sent, 0)
+        for r in range(2):
+            mix_copy((me + i) % GROUP, r).wait_send()
+        return carry
+
+    lax.fori_loop(1, GROUP, mix_sent, 0)
 
     def far_sent(h, carry):
         for r in range(2):
@@ -648,12 +690,13 @@
         pltpu.VMEM((2, 2, 128, 256), BF16),
         pltpu.VMEM((2, 2, 128, 256), BF16),
         pltpu.VMEM((2, ROWS, 128), F32),
+        pltpu.VMEM((GROUP, ROWS, 128), BF16),
         dma((GROUP,)),
         dma((GROUP,)),
         dma((11,)),
         dma((11,)),
-        dma((GROUP,)),
-        dma((GROUP,)),
+        dma((2 * GROUP,)),
+        dma((2 * GROUP,)),
         dma((2 * GROUP,)),
         dma((2 * GROUP,)),
         dma((4,)),
@@ -663,6 +706,8 @@
         dma((4,)),
         dma((4,)),
         dma((9,)),
+        pltpu.SemaphoreType.REGULAR,
+        pltpu.SemaphoreType.REGULAR,
     ]
     return pl.pallas_call(
         layer,

time: 51.7 us -> 47.8 us (0.925)
  the two profiles are of different devices: /device:TPU:34 before, /device:TPU:1 now
where the time goes in v3:
time: 47.8 us; the launch traced here: 47.6 us
  Pallas kernels  45.9 us (96%)
  local copies, waits for them, and re-layouts  1.67 us (3%)
    pallas_call x1, Pallas kernels, shards(): pl.pallas_call(layer, out_shape=jax.ShapeDtypeStruct((ROWS, COLS), BF16),...  45.9 us
    unnamed x1, local copies, waits for them, and re-layouts  1.67 us

profile of v3, /device:TPU:1, one launch (start us, length us, event | category | flops | bytes accessed | tf_op | source)
XLA Modules:
  0.0 47.6 jit_solution(9174192175239329394)
XLA Ops:
  0.0 45.9 %layer.1 = bf16[256,512]{1,0:T(8,128)(2,1)} custom-call(bf16[256,512]{1,0:T(8,128)(2,1)} %q_hbm.1, bf16[256,512]{1,0:T(8,128)(2,1)} %k_hbm.1, bf16[256,512]{1,0:T(8,128)(2,1)} %v_hbm.1, bf16[256,512]{1,0:T(8,128)(2,1)} %res_hbm.1, bf16[512,1024]{1,0:T(8,128)(2,1)} %out_hbm.1, f32[1,1024]{1,0:T(1,128)} %bitcast.1, s32[6,8]{1,0:T(8,128)} %offsets.1, ...), custom_call_target="tpu_custom_call" | custom-call | tf_op jit(solution)/shard_map/layer/pallas_call | solution.py:712
  45.9 1.7 %copy.12 = bf16[256,512]{1,0:T(8,128)(2,1)} copy(bf16[256,512]{1,0:T(8,128)(2,1)} %layer.1) | data formatting | bytes 524288

commit v4 on v3

--- a/solution.py
+++ b/solution.py
@@ -112,6 +112,10 @@
     local,
     here_sem,
     all_sem,
+    early_send,
+    early,
+    e_send,
+    e_got,
 ):
     seq = lax.axis_index("seq")
     tp = lax.axis_index("tp")
@@ -210,25 +214,43 @@
     def block_copy(to):
         return remote(send.at[to], got.at[me], a_send.at[to], a_got.at[me], (base + to, tp))
 
+    def pick_early(head):
+        wide = (64, ROWS)
+        i = sublanes(wide)
+        spot = jnp.full(wide, -1, jnp.int32)
+        for b, first, count in ((3, 0, 32), (4, 32, 16), (5, 48, 8)):
+            off = offsets[b, head] & (2**b - 1)
+            spot = jnp.where((i >= first) & (i < first + count), (i - first) * 2**b + off, spot)
+        rows = jnp.where(lanes(wide) == spot, 1.0, 0.0).astype(BF16)
+        early_send[head] = mm(rows, send[head, 0:ROWS]).astype(BF16)
+
+    def early_copy(to):
+        return remote(early_send.at[to], early.at[me], e_send.at[to], e_got.at[me], (base + to, tp))
+
+    def post(step, entered):
+        pair = (y + step) % 4
+        pack(pair)
+        for c in range(2):
+            pick_early(2 * pair + c)
+        entered()
+        for c in range(2):
+            early_copy(2 * pair + c).start()
+        for c in range(2):
+            block_copy(2 * pair + c).start()
+
     for load in loads[3:6]:
         load.wait()
-    pack((y + 2) % 4)
-    group_entered()
-
-    def post(step):
-        for c in range(2):
-            block_copy(((y + step) % 4) * 2 + c).start()
-
-    post(2)
-    pack((y + 1) % 4)
-    post(1)
-    pack((y + 3) % 4)
-    post(3)
+    post(2, group_entered)
+    post(1, lambda: None)
+    post(3, lambda: None)
     pack(y)
+    for c in range(2):
+        pick_early(2 * y + c)
+    early_copy(me + 1 - 2 * core).start()
     a_last = block_copy(me + 1 - 2 * core)
     a_last.start()
     got[me] = send[me]
-    all_entered()
+    early[me] = early_send[me]
 
     w_first = core * 128
     w_second = 256 + core * 128
@@ -239,9 +261,6 @@
 
     w_out = [w_piece(w_first, 0, partner, out_hbm), w_piece(w_second, 1, behind, out_hbm)]
     res_copy = remote(res_hbm, res_all.at[tp], r_send, r_got, partner)
-    res_copy.start()
-    for copy in w_out:
-        copy.start()
     for load in loads[0:3] + loads[6:]:
         load.start()
 
@@ -312,6 +331,34 @@
 
     def finish(o, top):
         return o + jnp.where(lanes(o.shape) == 1, top, 0.0)
+
+    all_entered()
+    res_copy.start()
+    for copy in w_out:
+        copy.start()
+
+    def early_wait(k, carry):
+        h = (me + k) % GROUP
+        remote(early_send.at[h], early.at[h], e_send.at[h], e_got.at[h], (base + h, tp)).wait_recv()
+        return carry
+
+    lax.fori_loop(1, GROUP, early_wait, 0)
+
+    def place(j, carry):
+        a = early[2 * j].astype(F32)
+        b = early[2 * j + 1].astype(F32)
+
+        def both(first, last):
+            return jnp.concatenate([a[first:last], b[first:last]], axis=0).astype(BF16)
+
+        k3[pl.ds(pl.multiple_of(z3 * 256 + j * 64, 64), 64)] = both(0, 32)
+        k4[pl.ds(pl.multiple_of(z4 * 128 + j * 32, 32), 32)] = both(32, 48)
+        k5[pl.ds(pl.multiple_of(z * 64 + j * 16, 16), 16)] = both(48, 56)
+        return carry
+
+    lax.fori_loop(0, GROUP // 2, place, 0)
+    all_known()
+    z_start()
 
     tri = lanes(square) <= sublanes(square)
 
@@ -363,17 +410,9 @@
         pick_kv[4 + j // 2, at] = both(0, 128, 192).astype(BF16)
         pick_v1[4 + j // 2, at] = with_ones(both(0, 128, 192))
         pick_q[4 + j // 2, at] = both(1, 128, 192).astype(BF16)
-        k3[pl.ds(pl.multiple_of(z3 * 256 + j * 64, 64), 64)] = both(0, 192, 224).astype(BF16)
         far_q[pl.ds(pl.multiple_of(j * 64, 64), 64)] = both(1, 192, 224).astype(BF16)
-        k4[pl.ds(pl.multiple_of(z4 * 128 + j * 32, 32), 32)] = both(0, 224, 240).astype(BF16)
         far_q[pl.ds(pl.multiple_of(256 + j * 32, 32), 32)] = both(1, 224, 240).astype(BF16)
-        k5[pl.ds(pl.multiple_of(z * 64 + j * 16, 16), 16)] = both(0, 240, 248).astype(BF16)
         far_q[pl.ds(pl.multiple_of(384 + j * 16, 16), 16)] = both(1, 240, 248).astype(BF16)
-
-        @pl.when(m == 3)
-        def _():
-            all_known()
-            z_start()
 
         o0, o1 = causal_pair(qs[0], qs[1], kvs[0], kvs[1], v1s[0], v1s[1])
         near_out[2 * j] = o0
@@ -502,36 +541,33 @@
 
     small = lanes((64, 128)) < 64
 
-    def weigh(s, carry):
+    for s in range(GROUP):
         mass = jnp.sum(jnp.where(lane // 16 == s, shares[1], 0.0), axis=1, keepdims=True)
-        weighed[s] = (pick_out[s] * mass).astype(BF16)
-        return carry
-
-    lax.fori_loop(0, GROUP, weigh, 0)
-
-    def combine(i, carry):
-        r = i // GROUP
-        s = (me + i + 3) % GROUP
-        rows = pl.ds(pl.multiple_of(128 * r, 128), 128)
-        near_share = jnp.sum(
-            jnp.where(lanes((128, 128)) == 16 * s, shares[0, rows], 0.0), axis=1, keepdims=True
-        )
-        both = near_out[s, rows] * near_share + mm(choose_t[rows], weighed[s])
-        mix = both / both[:, 0:1]
-        mix_send[s, r] = jnp.where(small, swap(mix[0:64]), mix[64:128]).astype(BF16)
-        far_copy(s, r).start()
-
-        @pl.when(s != me)
-        def _():
-            mix_copy(s, r).start()
-
-        @pl.when(s == me)
-        def _():
-            mix_own[me, r] = mix_send[me, r]
-
-        return carry
-
-    lax.fori_loop(0, 2 * GROUP, combine, 0)
+        weighed[:, 128 * s : 128 * s + 128] = (pick_out[s] * mass).astype(BF16)
+
+    for r in range(2):
+        rows = slice(128 * r, 128 * r + 128)
+        for pair in range(GROUP // 2):
+            more = mm(choose_t[rows], weighed[:, 256 * pair : 256 * pair + 256])
+            for c in range(2):
+                s = 2 * pair + c
+                both = near_out[s, rows] * shares[0, rows, 16 * s : 16 * s + 1]
+                both = both + more[:, 128 * c : 128 * c + 128]
+                mix = both / both[:, 0:1]
+                mix_send[s, r] = jnp.where(small, swap(mix[0:64]), mix[64:128]).astype(BF16)
+
+        def issue(i, carry):
+            s = (me + i + 3) % GROUP
+            far_copy(s, r).start()
+
+            @pl.when(s != me)
+            def _():
+                mix_copy(s, r).start()
+
+            return carry
+
+        lax.fori_loop(0, GROUP, issue, 0)
+        mix_own[me, r] = mix_send[me, r]
 
     def widen(blocks, r):
         for pair in range(GROUP // 2):
@@ -615,6 +651,7 @@
 
     def block_sent(k, carry):
         block_copy((me + k) % GROUP).wait_send()
+        early_copy((me + k) % GROUP).wait_send()
         return carry
 
     lax.fori_loop(1, GROUP, block_sent, 0)
@@ -690,7 +727,7 @@
         pltpu.VMEM((2, 2, 128, 256), BF16),
         pltpu.VMEM((2, 2, 128, 256), BF16),
         pltpu.VMEM((2, ROWS, 128), F32),
-        pltpu.VMEM((GROUP, ROWS, 128), BF16),
+        pltpu.VMEM((ROWS, GROUP * 128), BF16),
         dma((GROUP,)),
         dma((GROUP,)),
         dma((11,)),
@@ -708,6 +745,10 @@
         dma((9,)),
         pltpu.SemaphoreType.REGULAR,
         pltpu.SemaphoreType.REGULAR,
+        pltpu.VMEM((GROUP, 64, 128), BF16),
+        pltpu.VMEM((GROUP, 64, 128), BF16),
+        dma((GROUP,)),
+        dma((GROUP,)),
     ]
     return pl.pallas_call(
         layer,

time: 47.8 us -> 46.2 us (0.967)
  the two profiles are of different devices: /device:TPU:1 before, /device:TPU:34 now
where the time goes in v4:
time: 46.2 us; the launch traced here: 46.1 us
  Pallas kernels  44.4 us (96%)
  local copies, waits for them, and re-layouts  1.67 us (4%)
    pallas_call x1, Pallas kernels, shards(): pl.pallas_call(layer, out_shape=jax.ShapeDtypeStruct((ROWS, COLS), BF16),...  44.4 us
    unnamed x1, local copies, waits for them, and re-layouts  1.67 us

profile of v4, /device:TPU:34, one launch (start us, length us, event | category | flops | bytes accessed | tf_op | source)
XLA Modules:
  0.0 46.1 jit_solution(3553338049309401283)
XLA Ops:
  0.0 44.4 %layer.1 = bf16[256,512]{1,0:T(8,128)(2,1)} custom-call(bf16[256,512]{1,0:T(8,128)(2,1)} %q_hbm.1, bf16[256,512]{1,0:T(8,128)(2,1)} %k_hbm.1, bf16[256,512]{1,0:T(8,128)(2,1)} %v_hbm.1, bf16[256,512]{1,0:T(8,128)(2,1)} %res_hbm.1, bf16[512,1024]{1,0:T(8,128)(2,1)} %out_hbm.1, f32[1,1024]{1,0:T(1,128)} %bitcast.1, s32[6,8]{1,0:T(8,128)} %offsets.1, ...), custom_call_target="tpu_custom_call" | custom-call | tf_op jit(solution)/shard_map/layer/pallas_call | solution.py:753
  44.4 1.7 %copy.12 = bf16[256,512]{1,0:T(8,128)(2,1)} copy(bf16[256,512]{1,0:T(8,128)(2,1)} %layer.1) | data formatting | bytes 524288

commit v5 on v4

--- a/solution.py
+++ b/solution.py
@@ -177,6 +177,8 @@
         @pl.when(lead)
         def _():
             pl.semaphore_wait(here_sem, GROUP - 1)
+            for d in range(1, ZED):
+                greet((plane + ((z + d) % ZED) * GROUP, tp))
 
         @pl.when(me != 0)
         def _():
@@ -186,8 +188,6 @@
     def all_entered():
         @pl.when(lead)
         def _():
-            for d in range(1, ZED):
-                greet((plane + ((z + d) % ZED) * GROUP, tp))
             pl.semaphore_wait(barrier, ZED + 1)
             for k in range(1, GROUP):
                 pl.semaphore_signal(all_sem, inc=1, device_id=(base + k, tp), device_id_type=MESH)
@@ -559,14 +559,14 @@
         def issue(i, carry):
             s = (me + i + 3) % GROUP
             far_copy(s, r).start()
-
-            @pl.when(s != me)
-            def _():
-                mix_copy(s, r).start()
-
             return carry
 
+        def issue_own(i, carry):
+            mix_copy((me + i) % GROUP, r).start()
+            return carry
+
         lax.fori_loop(0, GROUP, issue, 0)
+        lax.fori_loop(1, GROUP, issue_own, 0)
         mix_own[me, r] = mix_send[me, r]
 
     def widen(blocks, r):

time: 46.2 us -> 45.6 us (0.987)
  Pallas kernels: 44.4 us -> 43.3 us
    pallas_call x1, Pallas kernels: 44.4 us -> 43.3 us  [shards(): pl.pallas_call(layer, out_shape=jax.ShapeDtypeStruct((ROWS, COLS), BF16),...]
where the time goes in v5:
time: 45.6 us; the launch traced here: 45 us
  Pallas kernels  43.3 us (95%)
  local copies, waits for them, and re-layouts  1.67 us (4%)
    pallas_call x1, Pallas kernels, shards(): pl.pallas_call(layer, out_shape=jax.ShapeDtypeStruct((ROWS, COLS), BF16),...  43.3 us
    unnamed x1, local copies, waits for them, and re-layouts  1.67 us

profile of v5, /device:TPU:34, one launch (start us, length us, event | category | flops | bytes accessed | tf_op | source)
XLA Modules:
  0.0 45.0 jit_solution(12431882222181964795)
XLA Ops:
  0.0 43.3 %layer.1 = bf16[256,512]{1,0:T(8,128)(2,1)} custom-call(bf16[256,512]{1,0:T(8,128)(2,1)} %q_hbm.1, bf16[256,512]{1,0:T(8,128)(2,1)} %k_hbm.1, bf16[256,512]{1,0:T(8,128)(2,1)} %v_hbm.1, bf16[256,512]{1,0:T(8,128)(2,1)} %res_hbm.1, bf16[512,1024]{1,0:T(8,128)(2,1)} %out_hbm.1, f32[1,1024]{1,0:T(1,128)} %bitcast.1, s32[6,8]{1,0:T(8,128)} %offsets.1, ...), custom_call_target="tpu_custom_call" | custom-call | tf_op jit(solution)/shard_map/layer/pallas_call | solution.py:753
  43.3 1.7 %copy.12 = bf16[256,512]{1,0:T(8,128)(2,1)} copy(bf16[256,512]{1,0:T(8,128)(2,1)} %layer.1) | data formatting | bytes 524288

commit v6 on v5

--- a/solution.py
+++ b/solution.py
@@ -427,8 +427,8 @@
     for copy in w_on:
         copy.start()
 
-    def picked(i, carry):
-        o0, o1 = causal_pair(
+    def picked(i):
+        return causal_pair(
             pick_q[2 * i],
             pick_q[2 * i + 1],
             pick_kv[2 * i],
@@ -437,22 +437,16 @@
             pick_v1[2 * i + 1],
         )
 
-        @pl.when(i < 2)
-        def _():
-            pick_out[4 * i, 0:128] = o0[0:128]
-            pick_out[4 * i + 1, 0:128] = o0[128:256]
-            pick_out[4 * i + 2, 0:128] = o1[0:128]
-            pick_out[4 * i + 3, 0:128] = o1[128:256]
-
-        @pl.when(i == 2)
-        def _():
-            for u in range(4):
-                pick_out[u, 128:192] = o0[64 * u : 64 * u + 64]
-                pick_out[4 + u, 128:192] = o1[64 * u : 64 * u + 64]
-
-        return carry
-
-    lax.fori_loop(0, 3, picked, 0)
+    for i in range(2):
+        o0, o1 = picked(i)
+        pick_out[4 * i, 0:128] = o0[0:128]
+        pick_out[4 * i + 1, 0:128] = o0[128:256]
+        pick_out[4 * i + 2, 0:128] = o1[0:128]
+        pick_out[4 * i + 3, 0:128] = o1[128:256]
+    o0, o1 = picked(2)
+    for u in range(4):
+        pick_out[u, 128:192] = o0[64 * u : 64 * u + 64]
+        pick_out[4 + u, 128:192] = o1[64 * u : 64 * u + 64]
 
     z_finish_got()
     for buffer, q_first, count, slot, first in (
@@ -638,6 +632,30 @@
 
     lax.fori_loop(0, 2, feed, 0)
 
+    def block_sent(k, carry):
+        block_copy((me + k) % GROUP).wait_send()
+        early_copy((me + k) % GROUP).wait_send()
+        return carry
+
+    lax.fori_loop(1, GROUP, block_sent, 0)
+    for copy in w_out + w_on + [res_copy]:
+        copy.wait_send()
+    z_finish_send()
+
+    def mix_sent(i, carry):
+        for r in range(2):
+            mix_copy((me + i) % GROUP, r).wait_send()
+        return carry
+
+    lax.fori_loop(1, GROUP, mix_sent, 0)
+
+    def far_sent(h, carry):
+        for r in range(2):
+            far_copy(h, r).wait_send()
+        return carry
+
+    lax.fori_loop(0, GROUP, far_sent, 0)
+
     def last(r, carry):
         rows = pl.ds(pl.multiple_of(128 * r, 128), 128)
         for n in range(2):
@@ -649,29 +667,6 @@
 
     lax.fori_loop(0, 2, last, 0)
 
-    def block_sent(k, carry):
-        block_copy((me + k) % GROUP).wait_send()
-        early_copy((me + k) % GROUP).wait_send()
-        return carry
-
-    lax.fori_loop(1, GROUP, block_sent, 0)
-    for copy in w_out + w_on + [res_copy]:
-        copy.wait_send()
-    z_finish_send()
-
-    def mix_sent(i, carry):
-        for r in range(2):
-            mix_copy((me + i) % GROUP, r).wait_send()
-        return carry
-
-    lax.fori_loop(1, GROUP, mix_sent, 0)
-
-    def far_sent(h, carry):
-        for r in range(2):
-            far_copy(h, r).wait_send()
-        return carry
-
-    lax.fori_loop(0, GROUP, far_sent, 0)
     for r in range(2):
         for n in range(2):
             down_copy(r, n).wait_send()

time: 45.6 us -> 45.2 us (level)
  no operation moved by 1% of the time
where the time goes in v6:
time: 45.2 us; the launch traced here: 44.7 us
  Pallas kernels  43 us (95%)
  local copies, waits for them, and re-layouts  1.67 us (4%)
    pallas_call x1, Pallas kernels, shards(): pl.pallas_call(layer, out_shape=jax.ShapeDtypeStruct((ROWS, COLS), BF16),...  43 us
    unnamed x1, local copies, waits for them, and re-layouts  1.67 us

profile of v6, /device:TPU:34, one launch (start us, length us, event | category | flops | bytes accessed | tf_op | source)
XLA Modules:
  0.0 44.7 jit_solution(16721101531384421421)
XLA Ops:
  0.0 43.0 %layer.1 = bf16[256,512]{1,0:T(8,128)(2,1)} custom-call(bf16[256,512]{1,0:T(8,128)(2,1)} %q_hbm.1, bf16[256,512]{1,0:T(8,128)(2,1)} %k_hbm.1, bf16[256,512]{1,0:T(8,128)(2,1)} %v_hbm.1, bf16[256,512]{1,0:T(8,128)(2,1)} %res_hbm.1, bf16[512,1024]{1,0:T(8,128)(2,1)} %out_hbm.1, f32[1,1024]{1,0:T(1,128)} %bitcast.1, s32[6,8]{1,0:T(8,128)} %offsets.1, ...), custom_call_target="tpu_custom_call" | custom-call | tf_op jit(solution)/shard_map/layer/pallas_call | solution.py:748
  43.0 1.7 %copy.12 = bf16[256,512]{1,0:T(8,128)(2,1)} copy(bf16[256,512]{1,0:T(8,128)(2,1)} %layer.1) | data formatting | bytes 524288

commit v7 on v6

--- a/solution.py
+++ b/solution.py
@@ -356,7 +356,8 @@
         k5[pl.ds(pl.multiple_of(z * 64 + j * 16, 16), 16)] = both(48, 56)
         return carry
 
-    lax.fori_loop(0, GROUP // 2, place, 0)
+    for j in range(GROUP // 2):
+        place(j, 0)
     all_known()
     z_start()
 

time: 45.2 us -> 45.2 us (level)
  no operation moved by 1% of the time
where the time goes in v7:
time: 45.2 us; the launch traced here: 44.7 us
  Pallas kernels  43 us (95%)
  local copies, waits for them, and re-layouts  1.67 us (4%)
    pallas_call x1, Pallas kernels, shards(): pl.pallas_call(layer, out_shape=jax.ShapeDtypeStruct((ROWS, COLS), BF16),...  43 us
    unnamed x1, local copies, waits for them, and re-layouts  1.67 us

profile of v7, /device:TPU:34, one launch (start us, length us, event | category | flops | bytes accessed | tf_op | source)
XLA Modules:
  0.0 44.7 jit_solution(18423652399846321248)
XLA Ops:
  0.0 43.0 %layer.1 = bf16[256,512]{1,0:T(8,128)(2,1)} custom-call(bf16[256,512]{1,0:T(8,128)(2,1)} %q_hbm.1, bf16[256,512]{1,0:T(8,128)(2,1)} %k_hbm.1, bf16[256,512]{1,0:T(8,128)(2,1)} %v_hbm.1, bf16[256,512]{1,0:T(8,128)(2,1)} %res_hbm.1, bf16[512,1024]{1,0:T(8,128)(2,1)} %out_hbm.1, f32[1,1024]{1,0:T(1,128)} %bitcast.1, s32[6,8]{1,0:T(8,128)} %offsets.1, ...), custom_call_target="tpu_custom_call" | custom-call | tf_op jit(solution)/shard_map/layer/pallas_call | solution.py:749
  43.0 1.7 %copy.12 = bf16[256,512]{1,0:T(8,128)(2,1)} copy(bf16[256,512]{1,0:T(8,128)(2,1)} %layer.1) | data formatting | bytes 524288
